TPU v7x, 32 devices: a whole 2x2x4 slice. The times are simulated.
32 devices in a mesh: lat: 8 (over z, x), chan: 4 (over y, core).
Axes of the slice: x: 2, y: 2, z: 4, core: 2. Of those that a mesh axis runs over, the one named last changes fastest.
Arguments:
- probe_field: bfloat16 [2, 384, 384, 1024], P(None, 'lat', 'chan'), may hold values from -6 to 6
- gate_slope: bfloat16 [384, 768, 1024], P('lat', None, 'chan'), may hold values from -0.099609375 to 1.09375
- spectral_filter: float32 [384, 384], P(None, 'chan'), may hold values from -4 to 4
- weight_in: bfloat16 [384, 768], replicated, may hold values from -0.3125 to 0.3125
- weight_out: bfloat16 [768, 384], replicated, may hold values from -0.21875 to 0.21875
- weight_flux: bfloat16 [384, 4], replicated, may hold values from -0.3125 to 0.3125
- send_cells: int32 [32, 8, 128], P(('lat', 'chan')), may hold values from 0 to 12287
- recv_slots: int32 [32, 4, 2048], P(('lat', 'chan')), may hold values from 0 to 1023
- recv_weights: float32 [32, 4, 2048], P(('lat', 'chan')), may hold values from 0.1 to 0.5
- ocean_probe: bfloat16 [2, 200, 64, 1024], P(None, None, 'lat', 'chan'), may hold values from -6 to 6
- ocean_mask: int32 [64, 1024], P('lat', 'chan'), may hold values 0 or 1
- coupling: bfloat16 [4, 200], replicated, may hold values from -3 to 3
- base_fine: bfloat16 [200, 64, 1024], P(None, 'lat', 'chan'), may hold values from -5 to 5
- sigma_fine: float32 [64, 1024], P('lat', 'chan'), may hold values from 0.5 to 2
- slope_fine: bfloat16 [800, 64, 1024], P(None, 'lat', 'chan'), may hold values from -0.099609375 to 1.09375
- gain_fine: float32 [200], replicated, may hold values from 0.1 to 1.9
- kernel_fine: float32 [200, 49], replicated, may hold values from -0.875 to 0.875
- expand_fine: bfloat16 [200, 800], replicated, may hold values from -0.4375 to 0.4375
- shrink_fine: bfloat16 [800, 200], replicated, may hold values from -0.21875 to 0.21875
- down_proj: bfloat16 [200, 250], replicated, may hold values from -0.4375 to 0.4375
- base_coarse: bfloat16 [250, 32, 512], P(None, 'lat', 'chan'), may hold values from -5 to 5
- sigma_coarse: float32 [32, 512], P('lat', 'chan'), may hold values from 0.5 to 2
- slope_coarse: bfloat16 [1000, 32, 512], P(None, 'lat', 'chan'), may hold values from -0.099609375 to 1.09375
- gain_coarse: float32 [250], replicated, may hold values from 0.1 to 1.9
- kernel_coarse: float32 [250, 49], replicated, may hold values from -0.875 to 0.875
- expand_coarse: bfloat16 [250, 1000], replicated, may hold values from -0.375 to 0.375
- shrink_coarse: bfloat16 [1000, 250], replicated, may hold values from -0.1875 to 0.1875
- up_proj: bfloat16 [250, 200], replicated, may hold values from -0.375 to 0.375
Outputs:
- atmos_out: bfloat16 [2, 384, 384, 1024], P(None, 'lat', 'chan')
- ocean_out: bfloat16 [2, 200, 64, 1024], P(None, None, 'lat', 'chan')
Inputs may be any that keep to these rules, and one draw needn't show every extreme that they name: `send_cells`: local cell numbers of a flux tile of 48 by 256 cells. `recv_slots`: slot numbers into the 8 times 128 received cells.
All inputs are finite; a program needn't handle non-finite values. No bound on the sum of `ocean_mask` on one device may be relied on, other than what follows from the above.
Results may differ from a plain program's by a relative error of at most 0.023.
Values may be sent and summed in bfloat16 or wider, within the bound.
No kernel may reach another device: no remote copies, remote signals or barrier semaphores. Data moves between devices by JAX's collectives and lax.ppermute only.
A program may use at most 256 MiB of HBM per device.

v0:
```python
import math

import jax
import jax.numpy as jnp
from jax import lax
from jax.sharding import PartitionSpec as P


def with_halo(block, sides, width):
    for axis, dim in sides:
        count = lax.axis_size(axis)
        forward = [(i, i + 1) for i in range(count - 1)]
        backward = [(target, source) for source, target in forward]
        low = lax.ppermute(
            lax.slice_in_dim(block, block.shape[dim] - width, None, axis=dim), axis, forward
        )
        high = lax.ppermute(lax.slice_in_dim(block, 0, width, axis=dim), axis, backward)
        block = jnp.concatenate([low, block, high], axis=dim)
    return block


def fourier_tables(count):
    column = jnp.arange(count, dtype=jnp.int32)
    half = count // 2
    wave = jnp.where(column <= half, column, column - half)
    points = jnp.arange(count, dtype=jnp.int32)
    phase = points[:, None] * wave[None, :] % count
    angles = phase.astype(jnp.float32) * (2.0 * math.pi / count)
    basis = jnp.where((column <= half)[None, :], jnp.cos(angles), jnp.sin(angles))
    forward = (basis / count).astype(jnp.bfloat16)
    factor = jnp.where((column == 0) | (column == half), 1.0, 2.0).astype(jnp.float32)
    inverse = (basis.T * factor[:, None]).astype(jnp.bfloat16)
    return (forward, inverse)


def cosine_tables(count):
    degree = jnp.arange(count, dtype=jnp.int32)
    points = jnp.arange(count, dtype=jnp.int32)
    phase = degree[None, :] * (2 * points[:, None] + 1) % (4 * count)
    basis = jnp.cos(phase.astype(jnp.float32) * (math.pi / (2 * count)))
    forward = (basis / count).astype(jnp.bfloat16)
    factor = jnp.where(degree == 0, 1.0, 2.0).astype(jnp.float32)
    inverse = (basis.T * factor[:, None]).astype(jnp.bfloat16)
    return (forward, inverse)


def depthwise(padded, kernel, rows, cols):
    total = jnp.zeros((padded.shape[0], padded.shape[1], rows, cols), jnp.float32)
    wide = padded.astype(jnp.float32)
    for offset in range(49):
        row_start = offset // 7
        col_start = offset % 7
        total = (
            total
            + wide[:, :, row_start : row_start + rows, col_start : col_start + cols]
            * kernel[:, offset][None, :, None, None]
        )
    return total


def level_tangent(field, padded, base, sigma, slope, gain, kernel, expand, shrink, mask_values):
    spread = depthwise(padded, kernel, field.shape[2], field.shape[3])
    center = jnp.mean(spread, axis=1, keepdims=True)
    normed = base.astype(jnp.float32)[None]
    along = jnp.mean(normed * spread, axis=1, keepdims=True)
    tangent = (
        gain[None, :, None, None] * sigma[None, None] * (spread - center - normed * along)
    ).astype(jnp.bfloat16)
    hidden = jnp.einsum("pqyx,qh->phyx", tangent, expand, preferred_element_type=jnp.float32)
    gated = (slope[None] * hidden).astype(jnp.bfloat16)
    output = jnp.einsum("phyx,hq->pqyx", gated, shrink, preferred_element_type=jnp.float32)
    return ((field.astype(jnp.float32) + output) * mask_values).astype(jnp.bfloat16)


def to_columns(mixed):
    return lax.all_to_all(mixed, "chan", split_axis=3, concat_axis=2, tiled=True)


def local(
    probe_field,
    gate_slope,
    spectral_filter,
    weight_in,
    weight_out,
    weight_flux,
    send_cells,
    recv_slots,
    recv_weights,
    ocean_probe,
    ocean_mask,
    coupling,
    base_fine,
    sigma_fine,
    slope_fine,
    gain_fine,
    kernel_fine,
    expand_fine,
    shrink_fine,
    down_proj,
    base_coarse,
    sigma_coarse,
    slope_coarse,
    gain_coarse,
    kernel_coarse,
    expand_coarse,
    shrink_coarse,
    up_proj,
):
    probe_count = probe_field.shape[0]
    band_rows = probe_field.shape[1]
    width_local = probe_field.shape[2]
    lon_count = probe_field.shape[3]
    lat_devices = lax.axis_size("lat")
    lat_count = band_rows * lat_devices
    mode_block = lon_count // lat_devices
    fwd_lon, inv_lon = fourier_tables(lon_count)
    fwd_lat, inv_lat = cosine_tables(lat_count)
    flux_rows = lax.dynamic_slice_in_dim(
        weight_flux, lax.axis_index("chan") * width_local, width_local, 0
    )
    fwd_blocks = fwd_lon.reshape(lon_count, lat_devices, mode_block)
    inv_blocks = inv_lon.reshape(lat_devices, mode_block, lon_count)
    fourier = jnp.einsum(
        "pncx,xam->pnacm", probe_field, fwd_blocks, preferred_element_type=jnp.float32
    )
    fourier = fourier.astype(jnp.bfloat16).reshape(
        probe_count, band_rows, lat_devices, width_local * mode_block
    )
    filter_wide = jnp.repeat(spectral_filter, mode_block, axis=1)
    gathered = lax.all_to_all(fourier, "lat", split_axis=2, concat_axis=1, tiled=True)
    spectrum = jnp.einsum("pnaj,nl->plaj", gathered, fwd_lat, preferred_element_type=jnp.float32)
    filtered = (spectrum * filter_wide[None, :, None, :]).astype(jnp.bfloat16)
    returned = lax.all_to_all(
        jnp.einsum("plaj,ln->pnaj", filtered, inv_lat, preferred_element_type=jnp.float32).astype(
            jnp.bfloat16
        ),
        "lat",
        split_axis=1,
        concat_axis=2,
        tiled=True,
    )
    returned = returned.reshape(probe_count, band_rows, lat_devices, width_local, mode_block)
    spatial = jnp.einsum(
        "pnacm,amx->pncx", returned, inv_blocks, preferred_element_type=jnp.float32
    )
    mixed = (probe_field.astype(jnp.float32) + spatial).astype(jnp.bfloat16)
    regrouped = to_columns(mixed)
    hidden = jnp.einsum("pncx,ch->pnhx", regrouped, weight_in, preferred_element_type=jnp.float32)
    gated = (gate_slope[None] * hidden).astype(jnp.bfloat16)
    update = jnp.einsum(
        "pnhx,hc->pncx", gated, weight_out, preferred_element_type=jnp.float32
    ).astype(jnp.bfloat16)
    update_back = lax.all_to_all(update, "chan", split_axis=2, concat_axis=3, tiled=True)
    result_field = probe_field.astype(jnp.float32) + update_back.astype(jnp.float32)
    atmos_out = result_field.astype(jnp.bfloat16)
    partial_flux = jnp.einsum(
        "pncx,cf->pfnx",
        result_field,
        flux_rows.astype(jnp.float32),
        precision=lax.Precision.HIGHEST,
    )
    flux_field = lax.psum_scatter(
        partial_flux.astype(jnp.bfloat16), "chan", scatter_dimension=3, tiled=True
    )
    flux_count = flux_field.shape[1]
    flat_tile = flux_field.reshape(probe_count, flux_count, -1)
    picked = jnp.take(flat_tile, send_cells.reshape(-1), axis=2)
    picked = picked.reshape(probe_count, flux_count, send_cells.shape[1], send_cells.shape[2])
    arrived = lax.all_to_all(picked, "lat", split_axis=2, concat_axis=2, tiled=True)
    pool_slots = arrived.reshape(probe_count, flux_count, -1)
    tile_rows = ocean_probe.shape[2]
    tile_cols = ocean_probe.shape[3]
    source_count = recv_slots.shape[1]
    taken = jnp.take(pool_slots, recv_slots.reshape(-1), axis=2)
    taken = taken.reshape(probe_count, flux_count, source_count, tile_rows * tile_cols)
    ocean_flux = jnp.sum(taken.astype(jnp.float32) * recv_weights[0][None, None], axis=2)
    ocean_flux = ocean_flux.reshape(probe_count, flux_count, tile_rows, tile_cols)
    mask_values = ocean_mask.astype(jnp.float32)
    forcing = jnp.einsum(
        "pfyx,fq->pqyx", ocean_flux, coupling.astype(jnp.float32), precision=lax.Precision.HIGHEST
    )
    start_field = ((ocean_probe.astype(jnp.float32) + forcing) * mask_values).astype(jnp.bfloat16)
    fine_padded = with_halo(start_field, (("lat", 2), ("chan", 3)), 3)
    level_one = level_tangent(
        start_field,
        fine_padded,
        base_fine,
        sigma_fine,
        slope_fine,
        gain_fine,
        kernel_fine,
        expand_fine,
        shrink_fine,
        mask_values,
    )
    fine_channels = level_one.shape[1]
    shaped = level_one.astype(jnp.float32).reshape(
        probe_count, fine_channels, tile_rows // 2, 2, tile_cols // 2, 2
    )
    pooled = jnp.mean(shaped, axis=(3, 5))
    coarse_field = jnp.einsum(
        "pqyx,qr->pryx", pooled, down_proj.astype(jnp.float32), precision=lax.Precision.HIGHEST
    ).astype(jnp.bfloat16)
    coarse_padded = with_halo(coarse_field, (("lat", 2), ("chan", 3)), 3)
    level_two = level_tangent(
        coarse_field,
        coarse_padded,
        base_coarse,
        sigma_coarse,
        slope_coarse,
        gain_coarse,
        kernel_coarse,
        expand_coarse,
        shrink_coarse,
        1.0,
    )
    raised = jnp.einsum("pryx,rq->pqyx", level_two, up_proj, preferred_element_type=jnp.float32)
    upsampled = jnp.repeat(jnp.repeat(raised, 2, axis=2), 2, axis=3)
    ocean_out = ((level_one.astype(jnp.float32) + upsampled) * mask_values).astype(jnp.bfloat16)
    return (atmos_out, ocean_out)


def solution(mesh):
    return jax.shard_map(
        local,
        mesh=mesh,
        in_specs=(
            P(None, "lat", "chan", None),
            P("lat", None, "chan"),
            P(None, "chan"),
            P(),
            P(),
            P(),
            P(("lat", "chan"), None, None),
            P(("lat", "chan"), None, None),
            P(("lat", "chan"), None, None),
            P(None, None, "lat", "chan"),
            P("lat", "chan"),
            P(),
            P(None, "lat", "chan"),
            P("lat", "chan"),
            P(None, "lat", "chan"),
            P(),
            P(),
            P(),
            P(),
            P(),
            P(None, "lat", "chan"),
            P("lat", "chan"),
            P(None, "lat", "chan"),
            P(),
            P(),
            P(),
            P(),
            P(),
        ),
        out_specs=(P(None, "lat", "chan", None), P(None, None, "lat", "chan")),
        check_vma=False,
    )
```

profile of v0, /device:TPU:9, one launch (start us, length us, event | category | flops | bytes accessed | tf_op | source)
XLA Modules:
  0.0 2286.8 jit_solution(6836467146145493602)
XLA Ops:
  7.2 17.0 fusion.308
  24.2 26.5 %convert_bitcast_fusion.2 = bf16[2,48,8,96,128]{4,3,1,0,2:T(8,128)(2,1)} fusion(bf16[2,48,96,1024]{3,2,1,0:T(8,128)(2,1)} %param.28, bf16[1024,8,128,1,1]{2,0,4,3,1:T(8,128)(2,1)S(1)} %fusion.308), kind=kOutput, calls=%fused_computation.23 | convolution fusion | flops 19336790016 | bytes 39845888 | tf_op jit(solution)/shard_map/pncx,xam->pnacm/dot_general | solution.py:123
  50.7 26.6 %reshape.408 = bf16[2,48,8,12288]{3,1,0,2:T(8,128)(2,1)} reshape(bf16[2,48,8,96,128]{4,3,1,0,2:T(8,128)(2,1)} %convert_bitcast_fusion.2) | data formatting | bytes 37748736 | tf_op jit(solution)/shard_map/reshape | solution.py:126
  89.0 18.4 copy.207
  110.0 379.7 %all-to-all-done = bf16[2,48,8,12288]{3,1,0,2:T(8,128)(2,1)} async-done(((bf16[2,48,8,12288]{3,1,0,2:T(8,128)(2,1)}), bf16[2,48,8,12288]{3,1,0,2:T(8,128)(2,1)}, u32[]{:S(2)}, u32[]{:S(2)}) %all-to-all-start) | async-done | bytes 18874400 | tf_op jit(solution)/shard_map/all_to_all | solution.py:130
  489.7 16.8 copy.142
  506.5 35.1 %fusion.15 = bf16[2,384,1,12288]{3,1,0,2:T(8,128)(2,1)} fusion(bf16[2,384,12288]{2,1,0:T(8,128)(2,1)} %bitcast.363, f32[384,12288]{1,0:T(8,128)} %bitcast.358, s32[384]{0:T(512)S(1)} %multiply_add_fusion.1, bf16[384,384,1]{0,1,2:T(8,128)(2,1)S(1)} %fusion.310), kind=kOutput, calls=%fused_computation.24 | convolution fusion | flops 14525448192 | bytes 56919552 | tf_op jit(solution)/shard_map/plaj,ln->pnaj/dot_general | solution.py:134
  541.6 34.7 %copy.144 = bf16[2,384,1,12288]{3,0,2,1:T(2,128)(2,1)} copy(bf16[2,384,1,12288]{3,1,0,2:T(8,128)(2,1)} %fusion.15) | data formatting | bytes 37748736 | tf_op jit(solution)/shard_map/convert_element_type | solution.py:134
  583.6 18.5 fusion.306
  602.1 387.5 %all-to-all-done.1 = bf16[2,384,1,12288]{3,0,2,1:T(2,128)(2,1)} async-done(((bf16[2,384,1,12288]{3,0,2,1:T(2,128)(2,1)}), bf16[2,384,1,12288]{3,0,2,1:T(2,128)(2,1)}, u32[]{:S(2)}, u32[]{:S(2)}) %all-to-all-start.1) | async-done | bytes 18874400 | tf_op jit(solution)/shard_map/all_to_all | solution.py:133
  989.6 16.5 copy.145
  1010.6 24.5 %fusion.13 = f32[2,48,96,1024,1]{3,2,0,1,4:T(8,128)} fusion(bf16[2,48,8,96,128]{4,3,1,0,2:T(8,128)(2,1)S(1)} %bitcast.366, bf16[8,128,1024,1,1]{2,1,3,4,0:T(8,128)(2,1)S(1)} %fusion.306), kind=kOutput, calls=%fused_computation.20 | convolution fusion | flops 19327352832 | bytes 58720256 | tf_op jit(solution)/shard_map/pnacm,amx->pncx/dot_general | solution.py:143
  1035.2 25.6 %fusion.1 = bf16[2,48,96,1024]{3,2,1,0:T(8,128)(2,1)} fusion(bf16[2,48,96,1024]{3,2,1,0:T(8,128)(2,1)} %param.28, f32[2,48,96,1024,1]{3,2,0,1,4:T(8,128)} %fusion.13), kind=kLoop, calls=%fused_computation.6 | loop fusion | flops 28311552 | bytes 75497472 | tf_op jit(solution)/shard_map/convert_element_type | solution.py:146
  1060.7 29.8 %copy.146 = bf16[2,48,96,1024]{2,1,0,3:T(8,128)(2,1)} copy(bf16[2,48,96,1024]{3,2,1,0:T(8,128)(2,1)} %fusion.1) | data formatting | bytes 37748736 | tf_op jit(solution)/shard_map/convert_element_type | solution.py:146
  1099.5 25.7 %copy.141 = f32[48,768,256]{1,2,0:T(8,128)} copy(bf16[48,768,256]{2,1,0:T(8,128)(2,1)} %param.29) | data formatting | bytes 56623104 | tf_op jit(solution)/shard_map/convert_element_type | solution.py:149
  1125.2 246.4 %all-to-all-done.2 = bf16[2,48,96,1024]{2,1,0,3:T(8,128)(2,1)} async-done(((bf16[2,48,96,1024]{2,1,0,3:T(8,128)(2,1)}), bf16[2,48,96,1024]{2,1,0,3:T(8,128)(2,1)}, u32[]{:S(2)}, u32[]{:S(2)}) %all-to-all-start.2) | async-done | bytes 18874400 | tf_op jit(solution)/shard_map/all_to_all | solution.py:76
  1371.6 30.8 %copy.190 = bf16[2,48,96,4,256]{4,3,2,1,0:T(4,128)(2,1)} copy(bf16[2,48,96,4,256]{2,1,0,4,3:T(8,128)(2,1)} %bitcast.20) | data formatting | bytes 37748736 | tf_op jit(solution)/shard_map/all_to_all | solution.py:76
  1402.3 18.3 copy.148
  1420.6 46.1 %convert_bitcast_fusion.1 = bf16[2,48,384,256]{2,3,1,0:T(8,128)(2,1)} fusion(f32[48,768,256]{1,2,0:T(8,128)} %copy.141, bf16[2,48,384,256]{3,2,1,0:T(8,128)(2,1)} %bitcast.367, bf16[768,384]{1,0:T(8,128)(2,1)S(1)} %copy-done, bf16[384,768]{1,0:T(8,128)(2,1)S(1)} %copy-done.79), kind=kOutput, calls=%fused_computation.22 | convolution fusion | flops 29038215168 | bytes 76677120 | tf_op jit(solution)/shard_map/pnhx,hc->pncx/dot_general | solution.py:150
  1466.7 24.4 %copy.150 = bf16[2,48,384,256]{3,1,0,2:T(8,128)(2,1)} copy(bf16[2,48,384,256]{2,3,1,0:T(8,128)(2,1)} %convert_bitcast_fusion.1) | data formatting | bytes 37748736 | tf_op jit(solution)/shard_map/convert_element_type | solution.py:152
  1499.6 204.7 %all-to-all-done.3 = bf16[2,48,384,256]{3,1,0,2:T(8,128)(2,1)} async-done(((bf16[2,48,384,256]{3,1,0,2:T(8,128)(2,1)}), bf16[2,48,384,256]{3,1,0,2:T(8,128)(2,1)}, u32[]{:S(2)}, u32[]{:S(2)}) %all-to-all-start.3) | async-done | bytes 18874400 | tf_op jit(solution)/shard_map/all_to_all | solution.py:153
  1704.2 20.4 copy.151
  1749.6 21.8 fusion.133
  1771.4 39.8 %copy.191 = bf16[2,4,48,1024]{1,2,0,3:T(8,128)(2,1)} copy(bf16[2,4,48,1024]{3,1,2,0:T(4,128)(2,1)S(1)} %fusion.133) | data formatting | bytes 1572864
  1811.2 46.2 %reshape.456 = bf16[1024,384]{1,0:T(8,128)(2,1)} reshape(bf16[1024,2,48,4]{3,2,1,0:T(8,128)(2,1)} %bitcast.359) | data formatting | bytes 1572864
  1858.2 22.9 %reduce-scatter.4.cloned.1.call-done = bf16[256,384]{1,0:T(8,128)(2,1)} async-done(((bf16[1024,384]{1,0:T(8,128)(2,1)}), bf16[256,384]{1,0:T(8,128)(2,1)}) %reduce-scatter.4.cloned.1.call-update) | async-done | bytes 196624
  1881.2 15.5 reshape.457
  1932.3 54.0 %gather_fusion.1 = bf16[8192,2,4]{2,1,0:T(2,128)(2,1)} fusion(bf16[2,4,1024]{1,0,2:T(2,128)(2,1)S(1)} %bitcast.373, s32[8192]{0:T(1024)S(1)} %broadcast_clamp_fusion), kind=kCustom, calls=%fused_computation.1 | custom fusion | bytes 294912 | tf_op jit(solution)/shard_map/jit(_take)/gather | solution.py:174
  1986.3 23.6 %multiply_reduce_fusion = f32[2,4,2048]{1,0,2:T(2,128)} fusion(bf16[2,4,4,2048]{1,0,3,2:T(2,128)(2,1)} %bitcast.372, pred[4,2048]{1,0:T(4,128)(4,1)S(1)} %compare_and_fusion, f32[4,2048]{1,0:T(4,128)S(1)} %bitcast.379), kind=kLoop, calls=%fused_computation.27 | loop fusion | flops 245760 | bytes 237568 | tf_op jit(solution)/shard_map/reduce_sum | solution.py:176
  2022.8 17.6 collective-permute-done
  2079.2 91.4 %fusion.265 = (f32[2,8,256]{2,1,0:T(8,128)S(1)}, f32[2,8,256]{2,1,0:T(8,128)S(1)}, f32[2,200,8,256]{3,1,2,0:T(8,128)}) fusion(f32[200,8,256]{2,0,1:T(8,128)S(1)} %copy-done.2, f32[200]{0:T(256)S(1)} %bitcast.478, f32[2,200,14,262]{3,1,2,0:T(8,128)} %maximum_convert_fusion, f32[200]{0:T(256)S(1)} %bitcast.479, f32[200]{0:T(256)S(1)} %bitcast.432, ...), kind=kLoop, calls=%fused_computation.383 | loop fusion | flops 81911808 | bytes 165550368 | tf_op jit(solution)/shard_map/reduce_sum | solution.py:63
  2222.1 25.6 %fusion.9 = bf16[2,48,96,1024]{3,2,1,0:T(8,128)(2,1)} fusion(f32[2,48,96,1024]{3,2,1,0:T(8,128)} %bitcast.357, bf16[2,48,96,1024]{3,2,1,0:T(8,128)(2,1)} %param.28), kind=kLoop, calls=%fused_computation.14 | loop fusion | flops 28311552 | bytes 75497472 | tf_op jit(solution)/shard_map/convert_element_type | solution.py:155
  (249 shorter events, 238.7 us)
Async XLA Ops:
  7.2 1413.5 %copy-start = (bf16[768,384]{1,0:T(8,128)(2,1)S(1)}, bf16[768,384]{1,0:T(8,128)(2,1)}, u32[]{:S(2)}) copy-start(bf16[768,384]{1,0:T(8,128)(2,1)} %param.32) | copy-start | bytes 1769476
  77.2 412.5 %all-to-all-start = ((bf16[2,48,8,12288]{3,1,0,2:T(8,128)(2,1)}), bf16[2,48,8,12288]{3,1,0,2:T(8,128)(2,1)}, u32[]{:S(2)}, u32[]{:S(2)}) async-start(bf16[2,48,8,12288]{3,1,0,2:T(8,128)(2,1)} %reshape.408), calls=%async_computation | async-start | bytes 37748736 | tf_op jit(solution)/shard_map/all_to_all | solution.py:130
  576.3 413.3 %all-to-all-start.1 = ((bf16[2,384,1,12288]{3,0,2,1:T(2,128)(2,1)}), bf16[2,384,1,12288]{3,0,2,1:T(2,128)(2,1)}, u32[]{:S(2)}, u32[]{:S(2)}) async-start(bf16[2,384,1,12288]{3,0,2,1:T(2,128)(2,1)} %copy.144), calls=%async_computation.1 | async-start | bytes 37748736 | tf_op jit(solution)/shard_map/all_to_all | solution.py:133
  1090.5 281.1 %all-to-all-start.2 = ((bf16[2,48,96,1024]{2,1,0,3:T(8,128)(2,1)}), bf16[2,48,96,1024]{2,1,0,3:T(8,128)(2,1)}, u32[]{:S(2)}, u32[]{:S(2)}) async-start(bf16[2,48,96,1024]{2,1,0,3:T(8,128)(2,1)} %copy.146), calls=%async_computation.2 | async-start | bytes 50331648 | tf_op jit(solution)/shard_map/all_to_all | solution.py:76
  1402.3 18.3 copy-start.79
  1491.1 8.4 copy-start.9
  1491.1 213.1 %all-to-all-start.3 = ((bf16[2,48,384,256]{3,1,0,2:T(8,128)(2,1)}), bf16[2,48,384,256]{3,1,0,2:T(8,128)(2,1)}, u32[]{:S(2)}, u32[]{:S(2)}) async-start(bf16[2,48,384,256]{3,1,0,2:T(8,128)(2,1)} %copy.150), calls=%async_computation.3 | async-start | bytes 37748736 | tf_op jit(solution)/shard_map/all_to_all | solution.py:153
  1499.5 381.7 %reduce-scatter.4.cloned.1.call-start = ((), (), s32[]{:S(2)}) async-start(), calls=%async_computation.6 | async-start | bytes 983040
  1811.2 46.3 %copy-start.15 = (s32[1,8,128]{2,1,0:T(8,128)S(1)}, s32[1,8,128]{2,1,0:T(8,128)}, u32[]{:S(2)}) copy-start(s32[1,8,128]{2,1,0:T(8,128)} %param.34) | copy-start | bytes 12292
  1811.2 46.3 %copy-start.12 = (f32[200,49]{0,1:T(8,128)S(1)}, f32[200,49]{0,1:T(8,128)}, u32[]{:S(2)}) copy-start(f32[200,49]{0,1:T(8,128)} %param.44) | copy-start | bytes 117604
  1904.7 23.6 %copy-start.17 = (s32[8,256]{1,0:T(8,128)S(1)}, s32[8,256]{1,0:T(8,128)}, u32[]{:S(2)}) copy-start(s32[8,256]{1,0:T(8,128)} %param.38) | copy-start | bytes 24580
  1904.7 81.6 %copy-start.14 = (f32[1,4,2048]{2,1,0:T(4,128)S(1)}, f32[1,4,2048]{2,1,0:T(4,128)}, u32[]{:S(2)}) copy-start(f32[1,4,2048]{2,1,0:T(4,128)} %param.36) | copy-start | bytes 98308
  1922.1 9.7 all-to-all-start.4
  1932.3 77.6 %copy-start.75 = (bf16[4,200]{1,0:T(4,128)(2,1)S(1)}, bf16[4,200]{1,0:T(4,128)(2,1)}, u32[]{:S(2)}) copy-start(bf16[4,200]{1,0:T(4,128)(2,1)} %param.39) | copy-start | bytes 4804
  2009.9 10.2 copy-start.13
  2009.9 11.5 copy-start.16
  2009.9 11.5 copy-start.78
  2013.9 26.5 %collective-permute-start = (bf16[2,200,3,256]{3,1,2,0:T(8,128)(2,1)S(1)}, bf16[2,200,3,256]{3,1,2,0:T(8,128)(2,1)S(1)}, u32[]{:S(2)}, u32[]{:S(2)}) collective-permute-start(bf16[2,200,3,256]{3,1,2,0:T(8,128)(2,1)S(1)} %get-tuple-element.22), channel_id=1, source_target_pairs={{0,4},{4,8},{8,12},{12,16},{16,20},{20,24},{24,28},{1,5},{5,9},{9,... | collective-permute-start | bytes 1843208 | tf_op jit(solution)/shard_map/ppermute | solution.py:14
  2016.2 29.5 %collective-permute-start.1 = (bf16[2,200,3,256]{3,1,2,0:T(8,128)(2,1)S(1)}, bf16[2,200,3,256]{3,1,2,0:T(8,128)(2,1)S(1)}, u32[]{:S(2)}, u32[]{:S(2)}) collective-permute-start(bf16[2,200,3,256]{3,1,2,0:T(8,128)(2,1)S(1)} %get-tuple-element.23), channel_id=1, source_target_pairs={{4,0},{8,4},{12,8},{16,12},{20,16},{24,20},{28,24},{5,1},{9,5},{13... | collective-permute-start | bytes 1843208 | tf_op jit(solution)/shard_map/ppermute | solution.py:17
  2050.1 17.8 collective-permute-start.2
  2054.4 15.2 collective-permute-start.3
  2071.2 7.6 copy-start.41
  2071.2 7.6 copy-start.42
  2071.2 7.6 copy-start.43
  2079.1 91.4 %copy-start.5 = (bf16[200,800]{1,0:T(8,128)(2,1)S(1)}, bf16[200,800]{1,0:T(8,128)(2,1)}, u32[]{:S(2)}) copy-start(bf16[200,800]{1,0:T(8,128)(2,1)} %param.45) | copy-start | bytes 960004
  2079.1 91.4 %copy-start.6 = (bf16[800,200]{0,1:T(8,128)(2,1)S(1)}, bf16[800,200]{0,1:T(8,128)(2,1)}, u32[]{:S(2)}) copy-start(bf16[800,200]{0,1:T(8,128)(2,1)} %param.46) | copy-start | bytes 960004
  2193.1 8.5 copy-start.76
  2193.1 8.5 copy-start.77
  2194.8 18.7 collective-permute-start.4
  2196.7 20.1 collective-permute-start.5
  2217.6 30.3 %collective-permute-start.6 = (bf16[2,250,10,3]{1,3,2,0:T(4,128)(2,1)S(1)}, bf16[2,250,10,3]{1,3,2,0:T(4,128)(2,1)S(1)}, u32[]{:S(2)}, u32[]{:S(2)}) collective-permute-start(bf16[2,250,10,3]{1,3,2,0:T(4,128)(2,1)S(1)} %get-tuple-element.24), channel_id=1, source_target_pairs={{0,1},{1,2},{2,3},{4,5},{5,6},{6,7},{8,9},{9,10},{10,11},{12,13},{... | collective-permute-start | bytes 90008 | tf_op jit(solution)/shard_map/ppermute | solution.py:14
  2220.2 27.8 %collective-permute-start.7 = (bf16[2,250,10,3]{1,3,2,0:T(4,128)(2,1)S(1)}, bf16[2,250,10,3]{1,3,2,0:T(4,128)(2,1)S(1)}, u32[]{:S(2)}, u32[]{:S(2)}) collective-permute-start(bf16[2,250,10,3]{1,3,2,0:T(4,128)(2,1)S(1)} %get-tuple-element.25), channel_id=1, source_target_pairs={{1,0},{2,1},{3,2},{5,4},{6,5},{7,6},{9,8},{10,9},{11,10},{13,12},{... | collective-permute-start | bytes 90008 | tf_op jit(solution)/shard_map/ppermute | solution.py:17
  (62 other events, 329.8 us)
Sparse Core Ops, SparseCore 0:
  1857.6 23.5 reduce-scatter.3
where the time goes:
time: 2300 us; the launch traced here: 2290 us
  waiting for transfers between devices  1280 us (56%)
  local copies, waits for them, and re-layouts  512 us (22%)
  other arithmetic  245 us (11%)
  matrix products  174 us (8%)
  starting transfers between devices  57.8 us (3%)
    all_to_all x1, waiting for transfers between devices, local(): lax.all_to_all(jnp.einsum('plaj,ln->pnaj', filtered, inv_lat, preferred_e...  388 us
    all_to_all x1, waiting for transfers between devices, local(): lax.all_to_all(fourier, 'lat', split_axis=2, concat_axis=1, tiled=True)  380 us
    all_to_all x1, waiting for transfers between devices, to_columns(): lax.all_to_all(mixed, 'chan', split_axis=3, concat_axis=2, tiled=True)  246 us
    all_to_all x1, waiting for transfers between devices, local(): lax.all_to_all(update, 'chan', split_axis=2, concat_axis=3, tiled=True)  205 us
    unnamed x169, local copies, waits for them, and re-layouts  135 us
    reduce_sum x2, other arithmetic, level_tangent(): center = jnp.mean(spread, axis=1, keepdims=True)  101 us
    gather x1, local copies, waits for them, and re-layouts, local(): taken = jnp.take(pool_slots, recv_slots.reshape(-1), axis=2)  54 us
    all_to_all x2, local copies, waits for them, and re-layouts, to_columns(): lax.all_to_all(mixed, 'chan', split_axis=3, concat_axis=2, tiled=True)  49.1 us
  transfers between devices with their start and end apart: 14, of which 10 were waited for; matrix products, arithmetic and copies ran while one was open for 5% of the time, Pallas kernels for 0%

commit v1 on v0

v1 whole, which is shorter than its diff:
```python
import functools
import math

import jax
import jax.numpy as jnp
from jax import lax
from jax.experimental import pallas as pl
from jax.experimental.pallas import tpu as pltpu
from jax.sharding import PartitionSpec as P

BF16 = jnp.bfloat16
F32 = jnp.float32
VMEM_BYTES = 56 * 1024 * 1024


def whole_spec(array):
    rank = array.ndim
    return pl.BlockSpec(array.shape, lambda *_: (0,) * rank)


def call(body, grid, in_specs, out_specs, out_shape, flops, moved, scratch=(), **extra):
    return pl.pallas_call(
        body,
        grid=grid,
        in_specs=in_specs,
        out_specs=out_specs,
        out_shape=out_shape,
        scratch_shapes=list(scratch),
        compiler_params=pltpu.CompilerParams(vmem_limit_bytes=VMEM_BYTES),
        cost_estimate=pl.CostEstimate(
            flops=int(flops), bytes_accessed=int(moved), transcendentals=0
        ),
        **extra,
    )


def dot(left, right):
    return jnp.dot(left, right, preferred_element_type=F32)


def tie(value, *others):
    others = jax.tree.leaves(others)
    anywhere = pl.BlockSpec(memory_space=pl.ANY)

    def body(*refs):
        pass

    return pl.pallas_call(
        body,
        in_specs=[anywhere] * (1 + len(others)),
        out_specs=anywhere,
        out_shape=jax.ShapeDtypeStruct(value.shape, value.dtype),
        input_output_aliases={0: 0},
        cost_estimate=pl.CostEstimate(flops=0, bytes_accessed=0, transcendentals=0),
    )(value, *others)


def cosine_tables(count):
    degree = jnp.arange(count, dtype=jnp.int32)
    points = jnp.arange(count, dtype=jnp.int32)
    phase = degree[None, :] * (2 * points[:, None] + 1) % (4 * count)
    basis = jnp.cos(phase.astype(F32) * (math.pi / (2 * count)))
    forward = (basis / count).astype(BF16)
    factor = jnp.where(degree == 0, 1.0, 2.0).astype(F32)
    inverse = (basis.T * factor[:, None]).astype(BF16)
    return (forward, inverse)


def with_halo(block, sides, width):
    for axis, dim in sides:
        count = lax.axis_size(axis)
        forward = [(i, i + 1) for i in range(count - 1)]
        backward = [(target, source) for source, target in forward]
        low = lax.ppermute(
            lax.slice_in_dim(block, block.shape[dim] - width, None, axis=dim), axis, forward
        )
        high = lax.ppermute(lax.slice_in_dim(block, 0, width, axis=dim), axis, backward)
        block = jnp.concatenate([low, block, high], axis=dim)
    return block


def mix_kernel(lat_devices, lon_blocks, field_ref, fwd_ref, inv_ref, filter_ref, *out_refs):
    rows, lanes = field_ref.shape[2:]
    width = out_refs[0].shape[3]
    for part, out_ref in enumerate(out_refs):
        starts = [(lon * len(out_refs) + part) * width for lon in range(lon_blocks)]
        block = jnp.concatenate(
            [field_ref[:, 0, :, start : start + width] for start in starts], axis=2
        )
        if rows % 16:
            block = block.astype(F32)
        field = block.reshape(lat_devices * rows, lon_blocks * width).astype(BF16)
        spectrum = dot(fwd_ref[...], field)
        filtered = (spectrum * filter_ref[0]).astype(BF16)
        mixed = field.astype(F32) + dot(inv_ref[...], filtered)
        for band in range(lat_devices):
            for lon in range(lon_blocks):
                out_ref[band * lon_blocks + lon, 0] = mixed[
                    band * rows : (band + 1) * rows, lon * width : (lon + 1) * width
                ].astype(BF16)


def mix_latitudes(gathered, fwd_rows, inv_rows, filters, lon_blocks, parts):
    lat_devices, channels, rows, lanes = gathered.shape
    width = lanes // (lon_blocks * parts)
    count = lat_devices * rows
    peers = lat_devices * lon_blocks
    return call(
        functools.partial(mix_kernel, lat_devices, lon_blocks),
        (channels,),
        [
            pl.BlockSpec((lat_devices, 1, rows, lanes), lambda c: (0, c, 0, 0)),
            whole_spec(fwd_rows),
            whole_spec(inv_rows),
            pl.BlockSpec((1, count, 1), lambda c: (c, 0, 0)),
        ],
        [pl.BlockSpec((peers, 1, rows, width), lambda c: (0, c, 0, 0))] * parts,
        [jax.ShapeDtypeStruct((peers, channels, rows, width), BF16)] * parts,
        4 * count * count * lanes * channels,
        4 * gathered.size,
    )(gathered, fwd_rows, inv_rows, filters)


def network_kernel(mixed_ref, slope_ref, win_ref, wout_ref, wflux_ref, flux_ref, *piece_refs):
    for row in range(mixed_ref.shape[0]):
        hidden = dot(win_ref[...], mixed_ref[row])
        gated = (slope_ref[row].astype(F32) * hidden).astype(BF16)
        update = dot(wout_ref[...], gated).astype(BF16)
        flux_ref[:, row] = dot(wflux_ref[...], update)
        width = piece_refs[0].shape[1]
        for index, piece_ref in enumerate(piece_refs):
            piece_ref[row] = update[index * width : (index + 1) * width]


def network(mixed, slope, part, win, wout, wflux, pieces):
    rows, channels, lanes = mixed.shape
    hidden = slope.shape[1]
    fluxes = wflux.shape[0]
    width = channels // pieces
    step = 8
    return call(
        network_kernel,
        (rows // step,),
        [
            pl.BlockSpec((step, channels, lanes), lambda n: (n, 0, 0)),
            pl.BlockSpec((step, hidden, lanes), lambda n: (n, 0, part)),
            whole_spec(win),
            whole_spec(wout),
            whole_spec(wflux),
        ],
        [pl.BlockSpec((fluxes, step, lanes), lambda n: (0, n, 0))]
        + [pl.BlockSpec((step, width, lanes), lambda n: (n, 0, 0))] * pieces,
        [jax.ShapeDtypeStruct((fluxes, rows, lanes), F32)]
        + [jax.ShapeDtypeStruct((rows, width, lanes), BF16)] * pieces,
        4 * rows * lanes * channels * hidden,
        2 * rows * lanes * (2 * channels + hidden),
    )(mixed, slope, win, wout, wflux)


def finish_kernel(parts, columns, place_ref, field_ref, *refs):
    out_ref = refs[-1]
    lanes = refs[0].shape[2]
    for index in range(parts * columns):
        part, shift = divmod(index, columns)
        block = lax.rem(place_ref[0] - shift + columns, columns)
        start = pl.multiple_of((block * parts + part) * lanes, lanes)
        span = pl.ds(start, lanes)
        out_ref[0, :, :, span] = (
            field_ref[0, :, :, span].astype(F32) + refs[index][...].astype(F32)
        ).astype(BF16)


def finish(probe, place, field, pieces, parts, columns, previous):
    rows, channels, lon_count = field.shape[1:]
    step = 4 if rows % 4 == 0 else 1
    block = pl.BlockSpec((1, step, channels, lon_count), lambda n: (probe, n, 0, 0))
    piece = pl.BlockSpec((step, channels, pieces[0].shape[2]), lambda n: (n, 0, 0))
    operands = [place, field, *pieces]
    specs = [pl.BlockSpec(memory_space=pltpu.SMEM), block] + [piece] * len(pieces)
    extra = {}
    if previous is not None:
        extra["input_output_aliases"] = {len(operands): 0}
        operands.append(previous)
        specs.append(pl.BlockSpec(memory_space=pl.ANY))
    return call(
        functools.partial(finish_kernel, parts, columns),
        (rows // step,),
        specs,
        block,
        jax.ShapeDtypeStruct(field.shape, BF16),
        field.size,
        6 * rows * channels * lon_count,
        **extra,
    )(*operands)


def pick_kernel(row_ref, col_ref, field_ref, *refs):
    part_refs, out_ref = refs[:-1], refs[-1]
    fields, rows, lanes = field_ref.shape
    cells = row_ref.shape[1]
    chosen = lax.broadcasted_iota(jnp.int32, (rows, cells), 0) == row_ref[...]
    chosen = jnp.where(chosen, 1.0, 0.0).astype(BF16)
    column = lax.broadcasted_iota(jnp.int32, (lanes, cells), 0) == col_ref[...]
    for field in range(fields):
        update = jnp.concatenate([part_ref[field] for part_ref in part_refs], axis=1)
        tile = (field_ref[field].astype(F32) + update).astype(BF16)
        lines = lax.dot_general(
            tile, chosen, (((0,), (0,)), ((), ())), preferred_element_type=F32
        )
        picked = jnp.sum(jnp.where(column, lines, 0.0), axis=0, keepdims=True).astype(BF16)
        count = out_ref.shape[2]
        for band in range(out_ref.shape[0]):
            out_ref[band, field : field + 1] = picked[:, band * count : (band + 1) * count]


def pick_cells(row, col, field, parts, bands):
    fields = field.shape[0]
    cells = row.shape[1]
    operands = (row, col, field, *parts)
    return call(
        pick_kernel,
        (1,),
        [whole_spec(operand) for operand in operands],
        pl.BlockSpec((bands, fields, cells // bands), lambda _: (0, 0, 0)),
        jax.ShapeDtypeStruct((bands, fields, cells // bands), BF16),
        4 * field.size * cells,
        8 * field.size,
    )(*operands)


def regrid_kernel(slot_ref, weight_ref, high_ref, low_ref):
    slots = high_ref.shape[1]
    lanes = high_ref.shape[2]
    number = lax.broadcasted_iota(jnp.int32, (slots, lanes), 0)
    total = jnp.zeros((slots, lanes), F32)
    for source in range(slot_ref.shape[1]):
        total = total + jnp.where(
            number == slot_ref[0, source : source + 1], weight_ref[0, source : source + 1], 0.0
        )
    high = total.astype(BF16)
    high_ref[0] = high
    low_ref[0] = (total - high.astype(F32)).astype(BF16)


def regrid_matrix(slot, weight, slots):
    rows, sources, lanes = slot.shape
    line = pl.BlockSpec((1, sources, lanes), lambda y: (y, 0, 0))
    table = pl.BlockSpec((1, slots, lanes), lambda y: (y, 0, 0))
    shape = jax.ShapeDtypeStruct((rows, slots, lanes), BF16)
    return call(
        regrid_kernel,
        (rows,),
        [line, line],
        [table, table],
        [shape, shape],
        12 * rows * slots * lanes,
        4 * rows * slots * lanes,
    )(slot, weight)


def start_kernel(pool_ref, high_ref, low_ref, coupling_ref, probe_ref, mask_ref, out_ref):
    pool = jnp.concatenate([pool_ref[band] for band in range(pool_ref.shape[0])], axis=1)
    flux = dot(pool, high_ref[0]) + dot(pool, low_ref[0])
    coupling = coupling_ref[...]
    total = probe_ref[0].astype(F32)
    for field in range(coupling.shape[1]):
        total = total + coupling[:, field : field + 1] * flux[field : field + 1]
    out_ref[0] = (total * mask_ref[0]).astype(BF16)


def start_level(pool, high, low, coupling, probe, mask):
    rows, channels, lanes = probe.shape
    slots = high.shape[1]
    table = pl.BlockSpec((1, slots, lanes), lambda y: (y, 0, 0))
    line = pl.BlockSpec((1, channels, lanes), lambda y: (y, 0, 0))
    return call(
        start_kernel,
        (rows,),
        [
            whole_spec(pool),
            table,
            table,
            whole_spec(coupling),
            line,
            pl.BlockSpec((1, 1, lanes), lambda y: (y, 0, 0)),
        ],
        line,
        jax.ShapeDtypeStruct(probe.shape, BF16),
        32 * high.size,
        4 * high.size,
    )(pool, high, low, coupling, probe, mask)


def spread_row(padded_ref, taps_ref, spread_ref, row, slot, lanes, chunk):
    channels = taps_ref.shape[1]
    tiles = padded_ref.shape[2] // 128

    def step(index, carry):
        span = pl.ds(pl.multiple_of(index * chunk, chunk), chunk)
        total = jnp.zeros((chunk, lanes), F32)
        for right in range(7):
            sums = [None] * tiles
            for down in range(7):
                tap = taps_ref[down * 7 + right, span, :]
                for tile in range(tiles):
                    term = padded_ref[row + down, span, tile * 128 : (tile + 1) * 128] * tap
                    sums[tile] = term if sums[tile] is None else sums[tile] + term
            line = jnp.concatenate(sums, axis=1)
            total = total + line[:, right : right + lanes]
        spread_ref[slot, span, :] = total
        return carry

    lax.fori_loop(0, channels // chunk, step, 0)


def tangent_row(spread, base, scale, count):
    center = jnp.sum(spread, axis=0, keepdims=True) / count
    along = jnp.sum(base * spread, axis=0, keepdims=True) / count
    return (scale * (spread - center - base * along)).astype(BF16)


def split_dot(left, right):
    high = right.astype(BF16)
    low = (right - high.astype(F32)).astype(BF16)
    return dot(left, high) + dot(left, low)


def fine_kernel(
    padded_ref,
    taps_ref,
    field_ref,
    base_ref,
    sigma_ref,
    slope_ref,
    gain_ref,
    expand_ref,
    shrink_ref,
    down_ref,
    pairs_ref,
    mask_ref,
    level_ref,
    coarse_ref,
    spread_ref,
):
    first = pl.program_id(0) * 2
    channels, lanes = field_ref.shape[1:]
    pooled = None
    for slot in range(2):
        spread_row(padded_ref, taps_ref, spread_ref, first + slot, slot, lanes, 40)
    for slot in range(2):
        tangent = tangent_row(
            spread_ref[slot],
            base_ref[slot].astype(F32),
            gain_ref[...] * sigma_ref[slot],
            channels,
        )
        hidden = dot(expand_ref[...], tangent)
        gated = (slope_ref[slot].astype(F32) * hidden).astype(BF16)
        output = dot(shrink_ref[...], gated)
        level = ((field_ref[slot].astype(F32) + output) * mask_ref[slot]).astype(BF16)
        level_ref[slot] = level
        share = dot(level, pairs_ref[...])
        pooled = share if pooled is None else pooled + share
    coarse_ref[0] = split_dot(down_ref[...], pooled).astype(BF16)


def fine_level(padded, taps, field, base, sigma, slope, gain, expand, shrink, down, pairs, mask):
    rows, channels, lanes = field.shape
    hidden = slope.shape[1]
    wide = down.shape[0]
    line = pl.BlockSpec((2, channels, lanes), lambda y: (y, 0, 0))
    thin = pl.BlockSpec((2, 1, lanes), lambda y: (y, 0, 0))
    return call(
        fine_kernel,
        (rows // 2,),
        [
            whole_spec(padded),
            whole_spec(taps),
            line,
            line,
            thin,
            pl.BlockSpec((2, hidden, lanes), lambda y: (y, 0, 0)),
            whole_spec(gain),
            whole_spec(expand),
            whole_spec(shrink),
            whole_spec(down),
            whole_spec(pairs),
            thin,
        ],
        [line, pl.BlockSpec((1, wide, lanes // 2), lambda y: (y, 0, 0))],
        [
            jax.ShapeDtypeStruct((rows, channels, lanes), BF16),
            jax.ShapeDtypeStruct((rows // 2, wide, lanes // 2), BF16),
        ],
        8 * rows * lanes * channels * hidden,
        4 * padded.size + 4 * taps.size + 2 * slope.size,
        scratch=[pltpu.VMEM((2, channels, lanes), F32)],
    )(padded, taps, field, base, sigma, slope, gain, expand, shrink, down, pairs, mask)


def coarse_kernel(
    count,
    padded_ref,
    taps_ref,
    field_ref,
    base_ref,
    sigma_ref,
    slope_ref,
    gain_ref,
    expand_ref,
    shrink_ref,
    up_ref,
    spread_out_ref,
    level_ref,
    mask_ref,
    out_ref,
    spread_ref,
):
    rows, _, lanes = field_ref.shape
    for row in range(rows):
        spread_row(padded_ref, taps_ref, spread_ref, row, row, lanes, 64)
    tangent = jnp.concatenate(
        [
            tangent_row(
                spread_ref[row],
                base_ref[row].astype(F32),
                gain_ref[...] * sigma_ref[row],
                count,
            )
            for row in range(rows)
        ],
        axis=1,
    )
    hidden = dot(expand_ref[...], tangent)
    gated = jnp.concatenate(
        [
            (slope_ref[row].astype(F32) * hidden[:, row * lanes : (row + 1) * lanes]).astype(BF16)
            for row in range(rows)
        ],
        axis=1,
    )
    output = dot(shrink_ref[...], gated)
    for row in range(rows):
        level = (
            field_ref[row].astype(F32) + output[:, row * lanes : (row + 1) * lanes]
        ).astype(BF16)
        raised = dot(up_ref[...], level)
        high = raised.astype(BF16)
        low = (raised - high.astype(F32)).astype(BF16)
        wide = dot(high, spread_out_ref[...]) + dot(low, spread_out_ref[...])
        for half in range(2):
            line = 2 * row + half
            out_ref[line] = ((level_ref[line].astype(F32) + wide) * mask_ref[line]).astype(BF16)


def coarse_level(
    count, padded, taps, field, base, sigma, slope, gain, expand, shrink, up, copies, level, mask
):
    operands = (
        padded,
        taps,
        field,
        base,
        sigma,
        slope,
        gain,
        expand,
        shrink,
        up,
        copies,
        level,
        mask,
    )
    return call(
        functools.partial(coarse_kernel, count),
        (1,),
        [whole_spec(operand) for operand in operands],
        whole_spec(level),
        jax.ShapeDtypeStruct(level.shape, BF16),
        8 * field.size * slope.shape[1],
        4 * padded.size + 4 * taps.size + 2 * slope.size + 4 * level.size,
        scratch=[pltpu.VMEM(field.shape, F32)],
    )(*operands)


def widen(array, dim, size):
    pads = [(0, 0)] * array.ndim
    pads[dim] = (0, size - array.shape[dim])
    return jnp.pad(array, pads)


def local(
    probe_field,
    gate_slope,
    spectral_filter,
    weight_in,
    weight_out,
    weight_flux,
    send_cells,
    recv_slots,
    recv_weights,
    ocean_probe,
    ocean_mask,
    coupling,
    base_fine,
    sigma_fine,
    slope_fine,
    gain_fine,
    kernel_fine,
    expand_fine,
    shrink_fine,
    down_proj,
    base_coarse,
    sigma_coarse,
    slope_coarse,
    gain_coarse,
    kernel_coarse,
    expand_coarse,
    shrink_coarse,
    up_proj,
):
    probes, rows, width, lon_count = probe_field.shape
    lat_devices = lax.axis_size("lat")
    columns = lax.axis_size("chan")
    lat_place = lax.axis_index("lat")
    place = lax.axis_index("chan")
    channels = width * columns
    group = width // lat_devices
    lon_block = lon_count // columns
    lanes = min(128, lon_block)
    parts = lon_block // lanes
    fluxes = weight_flux.shape[1]

    fwd_lat, inv_lat = cosine_tables(rows * lat_devices)
    fwd_rows, inv_rows = fwd_lat.T, inv_lat.T
    filters = lax.dynamic_slice_in_dim(spectral_filter, lat_place * group, group, 1).T[:, :, None]
    win = (
        weight_in.reshape(columns, lat_devices, group, -1)
        .transpose(3, 1, 0, 2)
        .reshape(-1, channels)
    )
    wout = jnp.roll(weight_out.T, -place * width, axis=0)
    wflux = jnp.roll(weight_flux.T, -place * width, axis=1)
    flux_rows = lax.dynamic_slice_in_dim(weight_flux, place * width, width, 0)

    flux_share = jnp.einsum(
        "pncx,cf->pfnx", probe_field, flux_rows, preferred_element_type=F32
    ).astype(BF16)
    flux_share = flux_share.reshape(probes * fluxes * rows, columns, lon_block).transpose(1, 0, 2)
    flux_field = lax.psum_scatter(flux_share, "chan", scatter_dimension=0, tiled=False)
    flux_field = flux_field.reshape(probes, fluxes, rows, lon_block)

    tile_rows, tile_cols = ocean_probe.shape[2:]
    slots = lat_devices * send_cells.shape[2]
    cells = send_cells.reshape(1, -1)
    cell_row, cell_col = cells // lon_block, cells % lon_block
    sources = recv_slots.shape[1]
    regrid_high, regrid_low = regrid_matrix(
        recv_slots.reshape(sources, tile_rows, tile_cols).transpose(1, 0, 2),
        recv_weights.reshape(sources, tile_rows, tile_cols).transpose(1, 0, 2),
        slots,
    )
    mask = ocean_mask.astype(F32)[:, None, :]
    ocean_start = ocean_probe.transpose(0, 2, 1, 3)
    coupling_rows = coupling.T.astype(F32)
    fine_count = kernel_fine.shape[0]
    coarse_count = kernel_coarse.shape[0]
    wide = -(-coarse_count // 64) * 64
    fine_args = (
        base_fine.transpose(1, 0, 2),
        sigma_fine[:, None, :],
        slope_fine.transpose(1, 0, 2),
        gain_fine[:, None],
        expand_fine.T,
        shrink_fine.T,
        widen(down_proj.T, 0, wide),
    )
    column = jnp.arange(tile_cols)
    pairs = jnp.where(column[:, None] // 2 == jnp.arange(tile_cols // 2)[None, :], 0.25, 0.0)
    pairs = pairs.astype(BF16)
    copies = jnp.where(jnp.arange(tile_cols // 2)[:, None] == column[None, :] // 2, 1.0, 0.0)
    copies = copies.astype(BF16)
    taps_fine = jnp.broadcast_to(kernel_fine.T[:, :, None], (49, fine_count, 128))
    taps_coarse = jnp.broadcast_to(
        widen(kernel_coarse, 0, wide).T[:, :, None], (49, wide, 128)
    )
    coarse_args = (
        widen(base_coarse.transpose(1, 0, 2), 1, wide),
        sigma_coarse[:, None, :],
        slope_coarse.transpose(1, 0, 2),
        widen(gain_coarse[:, None], 0, wide),
        widen(expand_coarse.T, 1, wide),
        widen(shrink_coarse.T, 0, wide),
        widen(up_proj.T, 1, wide),
        copies,
    )

    def send_field(probe):
        block = probe_field[probe].transpose(1, 0, 2)
        return block.reshape(lat_devices, group, rows, lon_count)

    def exchange(block, axes):
        return lax.all_to_all(block, axes, split_axis=0, concat_axis=0, tiled=True)

    def send_update(mixed, part):
        mixed = mixed.reshape(channels, rows, lanes).transpose(1, 0, 2)
        flux, *pieces = network(mixed, gate_slope, part, win, wout, wflux, columns)
        arrived = [pieces[0]]
        for shift in range(1, columns):
            pairs_of = [(source, (source + shift) % columns) for source in range(columns)]
            arrived.append(lax.ppermute(pieces[shift], "chan", pairs_of))
        return flux, arrived

    def ocean_start_field(probe, flux_parts, last):
        picked = pick_cells(cell_row, cell_col, flux_field[probe], flux_parts, lat_devices)
        if last:
            pool = exchange(picked, "lat")
        else:
            pool = lax.all_gather(picked, "lat", axis=0, tiled=False)
            pool = lax.dynamic_index_in_dim(pool, lat_place, 1, keepdims=False)
        return start_level(
            pool, regrid_high, regrid_low, coupling_rows, ocean_start[probe], mask
        )

    def ocean(start):
        padded = with_halo(start, (("lat", 0), ("chan", 2)), 3).astype(F32)
        padded = widen(padded, 2, tile_cols + 128)
        base, sigma, slope, gain, expand, shrink, down = fine_args
        level, coarse = fine_level(
            padded,
            taps_fine,
            start,
            base,
            sigma,
            slope,
            gain,
            expand,
            shrink,
            down,
            pairs,
            mask,
        )
        padded = with_halo(coarse, (("lat", 0), ("chan", 2)), 3).astype(F32)
        padded = widen(padded, 2, tile_cols // 2 + 128)
        return coarse_level(
            coarse_count, padded, taps_coarse, coarse, *coarse_args, level, mask
        )

    place_word = place.astype(jnp.int32).reshape(1)
    prepared = (
        flux_field,
        regrid_high,
        regrid_low,
        mask,
        ocean_start,
        coupling_rows,
        fine_args,
        coarse_args,
        pairs,
        taps_fine,
        taps_coarse,
        win,
        wout,
        wflux,
        cell_row,
        cell_col,
    )
    gathered = []
    for probe in range(probes):
        block = send_field(probe)
        if gathered:
            block = tie(block, gathered[-1], flux_share)
        gathered.append(exchange(block, "lat"))
    mixed = [
        mix_latitudes(block, fwd_rows, inv_rows, filters, columns, parts) for block in gathered
    ]
    order = [(probe, part) for probe in range(probes) for part in range(parts)]
    arrived = []
    updates = []
    starts = []

    def advance(block, *others):
        index = len(updates)
        if others:
            block = tie(block, *others)
        updates.append(send_update(block, order[index][1]))
        if (index + 1) % parts == 0:
            probe = index // parts
            flux_parts = [update[0] for update in updates[probe * parts :]]
            starts.append(ocean_start_field(probe, flux_parts, probe == probes - 1))

    def conclude(probe, previous):
        pieces = [
            piece for update in updates[probe * parts : (probe + 1) * parts] for piece in update[1]
        ]
        result = ocean(starts[probe])
        return result, finish(
            probe, place_word, probe_field, pieces, parts, columns, previous
        )

    for index, (probe, part) in enumerate(order):
        waits = [gathered[-1], prepared] if index == 0 else [arrived[-1]]
        if index == 1:
            waits += [mixed[-1]]
        if index >= 2:
            advance(arrived[index - 2])
            waits += [updates[-1][0], starts[-1:]]
        block = tie(mixed[probe][part], *waits)
        arrived.append(exchange(block, ("lat", "chan")))
    while len(updates) < len(order) - 1:
        advance(arrived[len(updates)])
    results = []
    atmos_out = None
    for probe in range(probes - 1):
        result, atmos_out = conclude(probe, atmos_out)
        results.append(result)
    advance(arrived[-1], results, atmos_out, updates[-1][0])
    result, atmos_out = conclude(probes - 1, atmos_out)
    results.append(result)
    return (atmos_out, jnp.stack(results).transpose(0, 2, 1, 3))


def solution(mesh):
    return jax.shard_map(
        local,
        mesh=mesh,
        in_specs=(
            P(None, "lat", "chan", None),
            P("lat", None, "chan"),
            P(None, "chan"),
            P(),
            P(),
            P(),
            P(("lat", "chan"), None, None),
            P(("lat", "chan"), None, None),
            P(("lat", "chan"), None, None),
            P(None, None, "lat", "chan"),
            P("lat", "chan"),
            P(),
            P(None, "lat", "chan"),
            P("lat", "chan"),
            P(None, "lat", "chan"),
            P(),
            P(),
            P(),
            P(),
            P(),
            P(None, "lat", "chan"),
            P("lat", "chan"),
            P(None, "lat", "chan"),
            P(),
            P(),
            P(),
            P(),
            P(),
        ),
        out_specs=(P(None, "lat", "chan", None), P(None, None, "lat", "chan")),
        check_vma=False,
    )
```

time: 2300 us -> 1400 us (0.61)
  waiting for transfers between devices: 1280 us -> 722 us
  local copies, waits for them, and re-layouts: 512 us -> 110 us
  Pallas kernels: 0 us -> 301 us
  other arithmetic: 245 us -> 26.6 us
  matrix products: 174 us -> 7.79 us
  blocking collectives: 0 us -> 81.7 us
  starting transfers between devices: 57.8 us -> 126 us
    all_to_all x5 -> x6, waiting for transfers between devices: 1220 us -> 472 us  [exchange(): return lax.all_to_all(block, axes, split_axis=0, concat_axis=0, tiled=True)]
    pallas_call x0 -> x23, Pallas kernels: none -> 301 us  [the longest x4 142 us: network(): call(network_kernel, (rows // step,), [pl.BlockSpec((step, channels, lane...]
    dot_general x10 -> x1, matrix products: 174 us -> 7.79 us  [local(): jnp.einsum('pncx,cf->pfnx', probe_field, flux_rows, preferred_element_typ...]
    convert_element_type x10 -> x2, local copies, waits for them, and re-layouts: 147 us -> 1.01 us  [the longest x1 0.77 us: local(): coupling_rows = coupling.T.astype(F32)]
    ppermute x0 -> x12, waiting for transfers between devices: none -> 143 us  [send_update(): arrived.append(lax.ppermute(pieces[shift], 'chan', pairs_of))]
    reduce_sum x4 -> x0, other arithmetic: 130 us -> none  [the longest x2 101 us: level_tangent(): center = jnp.mean(spread, axis=1, keepdims=True)]
    unnamed x169 -> x74, local copies, waits for them, and re-layouts: 135 us -> 12 us
    all_to_all x6 -> x0, local copies, waits for them, and re-layouts: 103 us -> none  [the longest x2 49.1 us: to_columns(): lax.all_to_all(mixed, 'chan', split_axis=3, concat_axis=2, tiled=True)]
  transfers between devices with their start and end apart: 14 -> 35, of which waited for: 10 -> 21; matrix products, arithmetic and copies ran while one was open for 5% -> 7% of each run, Pallas kernels for 0% -> 17%
where the time goes in v1:
time: 1400 us; the launch traced here: 1390 us
  waiting for transfers between devices  722 us (52%)
  Pallas kernels  301 us (22%)
  starting transfers between devices  126 us (9%)
  local copies, waits for them, and re-layouts  110 us (8%)
  blocking collectives  81.7 us (6%)
  other arithmetic  26.6 us (2%)
  between operations  15.1 us (1%)
    all_to_all x6, waiting for transfers between devices, exchange(): return lax.all_to_all(block, axes, split_axis=0, concat_axis=0, tiled=True)  472 us
    ppermute x12, waiting for transfers between devices, send_update(): arrived.append(lax.ppermute(pieces[shift], 'chan', pairs_of))  143 us
    pallas_call x4, Pallas kernels, network(): call(network_kernel, (rows // step,), [pl.BlockSpec((step, channels, lane...  142 us
    ppermute x8, waiting for transfers between devices, with_halo(): lax.ppermute(lax.slice_in_dim(block, block.shape[dim] - width, None, axis...  91.6 us
    all_gather x1, blocking collectives, ocean_start_field(): pool = lax.all_gather(picked, 'lat', axis=0, tiled=False)  71.4 us
    all_to_all x6, starting transfers between devices, exchange(): return lax.all_to_all(block, axes, split_axis=0, concat_axis=0, tiled=True)  48.1 us
    ppermute x8, starting transfers between devices, with_halo(): lax.ppermute(lax.slice_in_dim(block, block.shape[dim] - width, None, axis...  46.3 us
    pallas_call x2, Pallas kernels, fine_level(): call(fine_kernel, (rows // 2,), [whole_spec(padded), whole_spec(taps), li...  43.8 us
  transfers between devices with their start and end apart: 35, of which 21 were waited for; matrix products, arithmetic and copies ran while one was open for 7% of the time, Pallas kernels for 17%

profile of v1, /device:TPU:9, one launch (start us, length us, event | category | flops | bytes accessed | tf_op | source)
XLA Modules:
  0.0 1390.5 jit_solution(6238051752893698848)
XLA Ops:
  7.2 15.0 %slice_bitcast_fusion = (bf16[96,48,1024]{2,0,1:T(8,128)(2,1)}, bf16[96,48,1024]{2,0,1:T(8,128)(2,1)}) fusion(bf16[2,48,96,1024]{3,2,1,0:T(8,128)(2,1)} %field_ref.3), kind=kLoop, calls=%fused_computation | loop fusion | bytes 37748736 | tf_op jit(solution)/shard_map/transpose | solution.py:599
  22.2 12.6 copy.89
  50.3 12.7 copy.88
  63.1 181.4 %all-to-all-done.refs_1_.field_ref = bf16[8,12,48,1024]{3,2,1,0:T(8,128)(2,1)} async-done(((bf16[8,12,48,1024]{3,2,1,0:T(8,128)(2,1)}), bf16[8,12,48,1024]{3,2,1,0:T(8,128)(2,1)}, u32[]{:S(2)}, u32[]{:S(2)}) %all-to-all-start) | async-done | bytes 9437216 | tf_op jit(solution)/shard_map/all_to_all | solution.py:603
  290.4 18.3 %shard_map.277 = (bf16[32,12,48,128]{3,2,1,0:T(8,128)(2,1)}, bf16[32,12,48,128]{3,2,1,0:T(8,128)(2,1)}) custom-call(bf16[8,12,48,1024]{3,2,1,0:T(8,128)(2,1)} %all-to-all-done.refs_1_.field_ref, bf16[384,384]{1,0:T(8,128)(2,1)} %get-tuple-element.93.fwd_ref, bf16[384,384]{1,0:T(8,128)(2,1)} %get-tuple-element.92.inv_ref, f32[12,384,1]{2,1,0:T(8,128)} %copy.92.filter_ref), custom_call_target="tpu_custom_call" | custom-call | flops 7247757312 | bytes 18874368 | tf_op jit(solution)/shard_map/pallas_call | solution.py:108
  308.6 145.9 %all-to-all-done.1.field_ref.refs_1_ = bf16[8,12,48,1024]{3,2,1,0:T(8,128)(2,1)} async-done(((bf16[8,12,48,1024]{3,2,1,0:T(8,128)(2,1)}), bf16[8,12,48,1024]{3,2,1,0:T(8,128)(2,1)}, u32[]{:S(2)}, u32[]{:S(2)}) %all-to-all-start.1) | async-done | bytes 9437216 | tf_op jit(solution)/shard_map/all_to_all | solution.py:603
  468.0 18.2 %shard_map.276 = (bf16[32,12,48,128]{3,2,1,0:T(8,128)(2,1)}, bf16[32,12,48,128]{3,2,1,0:T(8,128)(2,1)}) custom-call(bf16[8,12,48,1024]{3,2,1,0:T(8,128)(2,1)} %all-to-all-done.1.field_ref.refs_1_, bf16[384,384]{1,0:T(8,128)(2,1)} %get-tuple-element.93.fwd_ref, bf16[384,384]{1,0:T(8,128)(2,1)} %get-tuple-element.92.inv_ref, f32[12,384,1]{2,1,0:T(8,128)} %copy.92.filter_ref), custom_call_target="tpu_custom_call" | custom-call | flops 7247757312 | bytes 18874368 | tf_op jit(solution)/shard_map/pallas_call | solution.py:108
  486.2 84.0 %all-to-all-done.2.refs_1_ = bf16[32,12,48,128]{3,2,1,0:T(8,128)(2,1)} async-done(((bf16[32,12,48,128]{3,2,1,0:T(8,128)(2,1)}), bf16[32,12,48,128]{3,2,1,0:T(8,128)(2,1)}, u32[]{:S(2)}, u32[]{:S(2)}) %all-to-all-start.2) | async-done | bytes 4718624 | tf_op jit(solution)/shard_map/all_to_all | solution.py:603
  570.3 9.3 all-to-all-start.3
  585.3 35.4 %shard_map.281 = (f32[4,48,128]{2,1,0:T(8,128)}, bf16[48,96,128]{2,1,0:T(8,128)(2,1)}, bf16[48,96,128]{2,1,0:T(8,128)(2,1)}, bf16[48,96,128]{2,1,0:T(8,128)(2,1)}, bf16[48,96,128]{2,1,0:T(8,128)(2,1)}) custom-call(bf16[48,384,128]{2,1,0:T(8,128)(2,1)} %bitcast.120, bf16[48,768,256]{2,1,0:T(8,128)(2,1)} %slope_ref.7, ...), custom_call_target="tpu_custom_call" | custom-call | flops 7247757312 | bytes 18874368 | tf_op jit(solution)/shard_map/pallas_call | solution.py:141
  620.7 61.0 %all-to-all-done.3.refs_1_ = bf16[32,12,48,128]{3,2,1,0:T(8,128)(2,1)} async-done(((bf16[32,12,48,128]{3,2,1,0:T(8,128)(2,1)}), bf16[32,12,48,128]{3,2,1,0:T(8,128)(2,1)}, u32[]{:S(2)}, u32[]{:S(2)}) %all-to-all-start.3) | async-done | bytes 4718624 | tf_op jit(solution)/shard_map/all_to_all | solution.py:603
  698.1 35.4 %shard_map.284 = (f32[4,48,128]{2,1,0:T(8,128)}, bf16[48,96,128]{2,1,0:T(8,128)(2,1)}, bf16[48,96,128]{2,1,0:T(8,128)(2,1)}, bf16[48,96,128]{2,1,0:T(8,128)(2,1)}, bf16[48,96,128]{2,1,0:T(8,128)(2,1)}) custom-call(bf16[48,384,128]{2,1,0:T(8,128)(2,1)} %bitcast.121, bf16[48,768,256]{2,1,0:T(8,128)(2,1)} %slope_ref.7, ...), custom_call_target="tpu_custom_call" | custom-call | flops 7247757312 | bytes 18874368 | tf_op jit(solution)/shard_map/pallas_call | solution.py:141
  735.9 71.4 %all-gather = bf16[64,4,128]{2,1,0:T(4,128)(2,1)S(1)} all-gather(bf16[8,4,128]{2,1,0:T(4,128)(2,1)} %shard_map.285), channel_id=2, replica_groups=mesh['lat'=8,'chan'=4] {'lat'}, dimensions={0}, use_global_device_ids=true | all-gather | bytes 73728 | tf_op jit(solution)/shard_map/all_gather | solution.py:619
  816.0 12.1 all-to-all-start.5
  834.5 80.7 %collective-permute-done.3 = bf16[3,200,256]{2,1,0:T(8,128)(2,1)S(1)} collective-permute-done((bf16[3,200,256]{2,1,0:T(8,128)(2,1)S(1)}, bf16[3,200,256]{2,1,0:T(8,128)(2,1)S(1)}, u32[]{:S(2)}, u32[]{:S(2)}) %collective-permute-start.3) | collective-permute-done | bytes 307232 | tf_op jit(solution)/shard_map/ppermute | solution.py:74
  932.4 21.9 %shard_map.288 = (bf16[8,200,256]{2,1,0:T(8,128)(2,1)}, bf16[4,256,128]{2,1,0:T(8,128)(2,1)}) custom-call(f32[14,200,384]{2,1,0:T(8,128)} %fusion.18.padded_ref, f32[49,200,128]{2,1,0:T(8,128)} %broadcast_in_dim.73.refs_24_.taps_ref, bf16[8,200,256]{2,1,0:T(8,128)(2,1)} %shard_map.286.refs_3_.field_ref, bf16[8,200,256]{2,1,0:T(8,128)(2,1)} %bitcast.111, ...), custom_call_target="tpu_custom_call" | custom-call | flops 2621440000 | bytes 12595200 | tf_op jit(solution)/shard_map/pallas_call | solution.py:373
  955.3 24.6 %collective-permute-start.7 = (bf16[3,256,128]{2,1,0:T(8,128)(2,1)S(1)}, bf16[3,256,128]{2,1,0:T(8,128)(2,1)S(1)}, u32[]{:S(2)}, u32[]{:S(2)}) collective-permute-start(bf16[3,256,128]{2,1,0:T(8,128)(2,1)S(1)} %get-tuple-element.89), channel_id=1, source_target_pairs={{0,4},{4,8},{8,12},{12,16},{16,20},{20,24},{24,28},{1,5},{5,9},{9,... | collective-permute-start | bytes 589832 | tf_op jit(solution)/shard_map/ppermute | solution.py:74
  1000.8 11.4 shard_map.289.refs_1_
  1012.1 10.2 collective-permute-done.12.refs_2_
  1022.3 24.2 %collective-permute-done.13.refs_3_ = bf16[48,96,128]{2,1,0:T(8,128)(2,1)} collective-permute-done((bf16[48,96,128]{2,1,0:T(8,128)(2,1)}, bf16[48,96,128]{2,1,0:T(8,128)(2,1)}, u32[]{:S(2)}, u32[]{:S(2)}) %collective-permute-start.13) | collective-permute-done | bytes 1179680 | tf_op jit(solution)/shard_map/ppermute | solution.py:611
  1046.5 26.4 %collective-permute-done.15.refs_6_ = bf16[48,96,128]{2,1,0:T(8,128)(2,1)} collective-permute-done((bf16[48,96,128]{2,1,0:T(8,128)(2,1)}, bf16[48,96,128]{2,1,0:T(8,128)(2,1)}, u32[]{:S(2)}, u32[]{:S(2)}) %collective-permute-start.15) | collective-permute-done | bytes 1179680 | tf_op jit(solution)/shard_map/ppermute | solution.py:611
  1073.0 11.9 collective-permute-done.16.refs_7_
  1084.9 14.1 %shard_map.290.refs_2_.refs_8_ = bf16[2,48,96,1024]{3,2,1,0:T(8,128)(2,1)} custom-call(s32[1]{0:T(128)} %bitcast.place_ref, bf16[2,48,96,1024]{3,2,1,0:T(8,128)(2,1)} %field_ref.3, bf16[48,96,128]{2,1,0:T(8,128)(2,1)} %get-tuple-element.46.refs_0_, bf16[48,96,128]{2,1,0:T(8,128)(2,1)} %collective-permute-done.11.refs_1_, bf16[48,96,128]{2,1,0:T(8,128)(2,1)} %copy-done.8, ...), custom_call_target="tpu_custom_call" | custom-call | flops 9437184 | bytes 28311552 | tf_op jit(solution)/shard_map/pallas_call | solution.py:185
  1104.8 35.4 %shard_map.283 = (f32[4,48,128]{2,1,0:T(8,128)}, bf16[48,96,128]{2,1,0:T(8,128)(2,1)}, bf16[48,96,128]{2,1,0:T(8,128)(2,1)}, bf16[48,96,128]{2,1,0:T(8,128)(2,1)}, bf16[48,96,128]{2,1,0:T(8,128)(2,1)}) custom-call(bf16[48,384,128]{2,1,0:T(8,128)(2,1)} %bitcast.122, bf16[48,768,256]{2,1,0:T(8,128)(2,1)} %slope_ref.7, ...), custom_call_target="tpu_custom_call" | custom-call | flops 7247757312 | bytes 18874368 | tf_op jit(solution)/shard_map/pallas_call | solution.py:141
  1146.0 35.6 %shard_map.292 = (f32[4,48,128]{2,1,0:T(8,128)}, bf16[48,96,128]{2,1,0:T(8,128)(2,1)}, bf16[48,96,128]{2,1,0:T(8,128)(2,1)}, bf16[48,96,128]{2,1,0:T(8,128)(2,1)}, bf16[48,96,128]{2,1,0:T(8,128)(2,1)}) custom-call(bf16[48,384,128]{2,1,0:T(8,128)(2,1)} %bitcast.119, bf16[48,768,256]{2,1,0:T(8,128)(2,1)} %slope_ref.7, ...), custom_call_target="tpu_custom_call" | custom-call | flops 7247757312 | bytes 18874368 | tf_op jit(solution)/shard_map/pallas_call | solution.py:141
  1184.0 10.3 all_to_all.35.pool_ref
  1237.2 21.9 %shard_map.296 = (bf16[8,200,256]{2,1,0:T(8,128)(2,1)}, bf16[4,256,128]{2,1,0:T(8,128)(2,1)}) custom-call(f32[14,200,384]{2,1,0:T(8,128)} %fusion.23.padded_ref, f32[49,200,128]{2,1,0:T(8,128)} %broadcast_in_dim.73.refs_24_.taps_ref, bf16[8,200,256]{2,1,0:T(8,128)(2,1)} %shard_map.295.field_ref, bf16[8,200,256]{2,1,0:T(8,128)(2,1)} %bitcast.112, ...), custom_call_target="tpu_custom_call" | custom-call | flops 2621440000 | bytes 12595200 | tf_op jit(solution)/shard_map/pallas_call | solution.py:373
  1284.7 11.4 shard_map.297
  1306.0 25.1 %collective-permute-done.2.refs_3_ = bf16[48,96,128]{2,1,0:T(8,128)(2,1)} collective-permute-done((bf16[48,96,128]{2,1,0:T(8,128)(2,1)}, bf16[48,96,128]{2,1,0:T(8,128)(2,1)}, u32[]{:S(2)}, u32[]{:S(2)}) %collective-permute-start.2) | collective-permute-done | bytes 1179680 | tf_op jit(solution)/shard_map/ppermute | solution.py:611
  1331.1 25.6 %collective-permute-done.18.refs_6_ = bf16[48,96,128]{2,1,0:T(8,128)(2,1)} collective-permute-done((bf16[48,96,128]{2,1,0:T(8,128)(2,1)}, bf16[48,96,128]{2,1,0:T(8,128)(2,1)}, u32[]{:S(2)}, u32[]{:S(2)}) %collective-permute-start.18) | collective-permute-done | bytes 1179680 | tf_op jit(solution)/shard_map/ppermute | solution.py:611
  1356.7 12.3 collective-permute-done.19.refs_7_
  1369.0 14.2 %shard_map.293 = bf16[2,48,96,1024]{3,2,1,0:T(8,128)(2,1)} custom-call(s32[1]{0:T(128)} %bitcast.place_ref, bf16[2,48,96,1024]{3,2,1,0:T(8,128)(2,1)} %field_ref.3, bf16[48,96,128]{2,1,0:T(8,128)(2,1)} %get-tuple-element.39.refs_0_, bf16[48,96,128]{2,1,0:T(8,128)(2,1)} %collective-permute-done.refs_1_, ...), custom_call_target="tpu_custom_call", output_to_operand_aliasing={{}: (10, {})} | custom-call | flops 9437184 | bytes 28311552 | tf_op jit(solution)/shard_map/pallas_call | solution.py:185
  (216 shorter events, 245.6 us)
Async XLA Ops:
  34.8 209.7 %all-to-all-start = ((bf16[8,12,48,1024]{3,2,1,0:T(8,128)(2,1)}), bf16[8,12,48,1024]{3,2,1,0:T(8,128)(2,1)}, u32[]{:S(2)}, u32[]{:S(2)}) async-start(bf16[8,12,48,1024]{3,2,1,0:T(8,128)(2,1)} %bitcast.104), calls=%async_computation | async-start | bytes 18874368 | tf_op jit(solution)/shard_map/all_to_all | solution.py:603
  244.5 210.0 %all-to-all-start.1 = ((bf16[8,12,48,1024]{3,2,1,0:T(8,128)(2,1)}), bf16[8,12,48,1024]{3,2,1,0:T(8,128)(2,1)}, u32[]{:S(2)}, u32[]{:S(2)}) async-start(bf16[8,12,48,1024]{3,2,1,0:T(8,128)(2,1)} %shard_map.275), calls=%async_computation.1 | async-start | bytes 18874368 | tf_op jit(solution)/shard_map/all_to_all | solution.py:603
  250.5 58.1 %reduce-scatter.2.cloned.1.call-start = ((), (), s32[]{:S(2)}) async-start(), calls=%async_computation.8 | async-start | bytes 983040 | tf_op jit(solution)/shard_map/reduce_scatter | solution.py:550
  461.9 108.4 %all-to-all-start.2 = ((bf16[32,12,48,128]{3,2,1,0:T(8,128)(2,1)}), bf16[32,12,48,128]{3,2,1,0:T(8,128)(2,1)}, u32[]{:S(2)}, u32[]{:S(2)}) async-start(bf16[32,12,48,128]{3,2,1,0:T(8,128)(2,1)} %shard_map.279), calls=%async_computation.3 | async-start | bytes 9437184 | tf_op jit(solution)/shard_map/all_to_all | solution.py:603
  570.3 111.4 %all-to-all-start.3 = ((bf16[32,12,48,128]{3,2,1,0:T(8,128)(2,1)}), bf16[32,12,48,128]{3,2,1,0:T(8,128)(2,1)}, u32[]{:S(2)}, u32[]{:S(2)}) async-start(bf16[32,12,48,128]{3,2,1,0:T(8,128)(2,1)} %shard_map.280), calls=%async_computation.4 | async-start | bytes 9437184 | tf_op jit(solution)/shard_map/all_to_all | solution.py:603
  681.6 134.4 %all-to-all-start.4 = ((bf16[32,12,48,128]{3,2,1,0:T(8,128)(2,1)}), bf16[32,12,48,128]{3,2,1,0:T(8,128)(2,1)}, u32[]{:S(2)}, u32[]{:S(2)}) async-start(bf16[32,12,48,128]{3,2,1,0:T(8,128)(2,1)} %shard_map.282), calls=%async_computation.5 | async-start | bytes 9437184 | tf_op jit(solution)/shard_map/all_to_all | solution.py:603
  816.0 324.2 %all-to-all-start.5 = ((bf16[32,12,48,128]{3,2,1,0:T(8,128)(2,1)}), bf16[32,12,48,128]{3,2,1,0:T(8,128)(2,1)}, u32[]{:S(2)}, u32[]{:S(2)}) async-start(bf16[32,12,48,128]{3,2,1,0:T(8,128)(2,1)} %shard_map.287), calls=%async_computation.6 | async-start | bytes 9437184 | tf_op jit(solution)/shard_map/all_to_all | solution.py:603
  828.2 87.1 %collective-permute-start.3 = (bf16[3,200,256]{2,1,0:T(8,128)(2,1)S(1)}, bf16[3,200,256]{2,1,0:T(8,128)(2,1)S(1)}, u32[]{:S(2)}, u32[]{:S(2)}) collective-permute-start(bf16[3,200,256]{2,1,0:T(8,128)(2,1)S(1)} %get-tuple-element.80), channel_id=1, source_target_pairs={{0,4},{4,8},{8,12},{12,16},{16,20},{20,24},{24,28},{1,5},{5,9},{9,... | collective-permute-start | bytes 921608 | tf_op jit(solution)/shard_map/ppermute | solution.py:74
  831.3 84.0 %collective-permute-start.4 = (bf16[3,200,256]{2,1,0:T(8,128)(2,1)S(1)}, bf16[3,200,256]{2,1,0:T(8,128)(2,1)S(1)}, u32[]{:S(2)}, u32[]{:S(2)}) collective-permute-start(bf16[3,200,256]{2,1,0:T(8,128)(2,1)S(1)} %get-tuple-element.81), channel_id=1, source_target_pairs={{4,0},{8,4},{12,8},{16,12},{20,16},{24,20},{28,24},{5,1},{9,5},{13... | collective-permute-start | bytes 921608 | tf_op jit(solution)/shard_map/ppermute | solution.py:77
  916.2 9.1 collective-permute-start.5
  923.5 71.4 %collective-permute-start.11 = (bf16[48,96,128]{2,1,0:T(8,128)(2,1)}, bf16[48,96,128]{2,1,0:T(8,128)(2,1)}, u32[]{:S(2)}, u32[]{:S(2)}) collective-permute-start(bf16[48,96,128]{2,1,0:T(8,128)(2,1)} %get-tuple-element.47), channel_id=1, source_target_pairs={{0,1},{1,2},{2,3},{3,0},{4,5},{5,6},{6,7},{7,4},{8,9},{9,10},{10,1... | collective-permute-start | bytes 3538952 | tf_op jit(solution)/shard_map/ppermute | solution.py:611
  955.3 27.2 %collective-permute-start.7 = (bf16[3,256,128]{2,1,0:T(8,128)(2,1)S(1)}, bf16[3,256,128]{2,1,0:T(8,128)(2,1)S(1)}, u32[]{:S(2)}, u32[]{:S(2)}) collective-permute-start(bf16[3,256,128]{2,1,0:T(8,128)(2,1)S(1)} %get-tuple-element.89), channel_id=1, source_target_pairs={{0,4},{4,8},{8,12},{12,16},{16,20},{20,24},{24,28},{1,5},{5,9},{9,... | collective-permute-start | bytes 589832 | tf_op jit(solution)/shard_map/ppermute | solution.py:74
  979.9 8.0 collective-permute-start.8
  988.5 7.7 collective-permute-start.10
  990.7 6.9 collective-permute-start.9
  994.4 27.9 %collective-permute-start.12 = (bf16[48,96,128]{2,1,0:T(8,128)(2,1)}, bf16[48,96,128]{2,1,0:T(8,128)(2,1)S(1)}, u32[]{:S(2)}, u32[]{:S(2)}) collective-permute-start(bf16[48,96,128]{2,1,0:T(8,128)(2,1)} %get-tuple-element.48), channel_id=1, source_target_pairs={{0,2},{1,3},{2,0},{3,1},{4,6},{5,7},{6,4},{7,5},{8,10},{9,11},{10,... | collective-permute-start | bytes 3538952 | tf_op jit(solution)/shard_map/ppermute | solution.py:611
  994.5 52.1 %collective-permute-start.13 = (bf16[48,96,128]{2,1,0:T(8,128)(2,1)}, bf16[48,96,128]{2,1,0:T(8,128)(2,1)}, u32[]{:S(2)}, u32[]{:S(2)}) collective-permute-start(bf16[48,96,128]{2,1,0:T(8,128)(2,1)} %get-tuple-element.49), channel_id=1, source_target_pairs={{0,3},{1,0},{2,1},{3,2},{4,7},{5,4},{6,5},{7,6},{8,11},{9,8},{10,9... | collective-permute-start | bytes 3538952 | tf_op jit(solution)/shard_map/ppermute | solution.py:611
  994.9 51.7 %collective-permute-start.14 = (bf16[48,96,128]{2,1,0:T(8,128)(2,1)}, bf16[48,96,128]{2,1,0:T(8,128)(2,1)}, u32[]{:S(2)}, u32[]{:S(2)}) collective-permute-start(bf16[48,96,128]{2,1,0:T(8,128)(2,1)} %get-tuple-element.51), channel_id=1, source_target_pairs={{0,1},{1,2},{2,3},{3,0},{4,5},{5,6},{6,7},{7,4},{8,9},{9,10},{10,1... | collective-permute-start | bytes 3538952 | tf_op jit(solution)/shard_map/ppermute | solution.py:611
  996.3 76.7 %collective-permute-start.15 = (bf16[48,96,128]{2,1,0:T(8,128)(2,1)}, bf16[48,96,128]{2,1,0:T(8,128)(2,1)}, u32[]{:S(2)}, u32[]{:S(2)}) collective-permute-start(bf16[48,96,128]{2,1,0:T(8,128)(2,1)} %get-tuple-element.52), channel_id=1, source_target_pairs={{0,2},{1,3},{2,0},{3,1},{4,6},{5,7},{6,4},{7,5},{8,10},{9,11},{10,... | collective-permute-start | bytes 3538952 | tf_op jit(solution)/shard_map/ppermute | solution.py:611
  997.7 87.2 %collective-permute-start.16 = (bf16[48,96,128]{2,1,0:T(8,128)(2,1)}, bf16[48,96,128]{2,1,0:T(8,128)(2,1)}, u32[]{:S(2)}, u32[]{:S(2)}) collective-permute-start(bf16[48,96,128]{2,1,0:T(8,128)(2,1)} %get-tuple-element.53), channel_id=1, source_target_pairs={{0,3},{1,0},{2,1},{3,2},{4,7},{5,4},{6,5},{7,6},{8,11},{9,8},{10,9... | collective-permute-start | bytes 3538952 | tf_op jit(solution)/shard_map/ppermute | solution.py:611
  1203.5 15.2 %collective-permute-start.20 = (bf16[3,200,256]{2,1,0:T(8,128)(2,1)S(1)}, bf16[3,200,256]{2,1,0:T(8,128)(2,1)S(1)}, u32[]{:S(2)}, u32[]{:S(2)}) collective-permute-start(bf16[3,200,256]{2,1,0:T(8,128)(2,1)S(1)} %get-tuple-element.78), channel_id=1, source_target_pairs={{0,4},{4,8},{8,12},{12,16},{16,20},{20,24},{24,28},{1,5},{5,9},{9,... | collective-permute-start | bytes 921608 | tf_op jit(solution)/shard_map/ppermute | solution.py:74
  1205.8 16.2 %collective-permute-start.21 = (bf16[3,200,256]{2,1,0:T(8,128)(2,1)S(1)}, bf16[3,200,256]{2,1,0:T(8,128)(2,1)S(1)}, u32[]{:S(2)}, u32[]{:S(2)}) collective-permute-start(bf16[3,200,256]{2,1,0:T(8,128)(2,1)S(1)} %get-tuple-element.79), channel_id=1, source_target_pairs={{4,0},{8,4},{12,8},{16,12},{20,16},{24,20},{28,24},{5,1},{9,5},{13... | collective-permute-start | bytes 921608 | tf_op jit(solution)/shard_map/ppermute | solution.py:77
  1224.1 6.6 collective-permute-start.22
  1228.9 49.7 %collective-permute-start = (bf16[48,96,128]{2,1,0:T(8,128)(2,1)}, bf16[48,96,128]{2,1,0:T(8,128)(2,1)}, u32[]{:S(2)}, u32[]{:S(2)}) collective-permute-start(bf16[48,96,128]{2,1,0:T(8,128)(2,1)} %get-tuple-element.40), channel_id=1, source_target_pairs={{0,1},{1,2},{2,3},{3,0},{4,5},{5,6},{6,7},{7,4},{8,9},{9,10},{10,1... | collective-permute-start | bytes 3538952 | tf_op jit(solution)/shard_map/ppermute | solution.py:611
  1260.2 7.4 collective-permute-start.24
  1262.2 9.5 collective-permute-start.25
  1272.3 7.7 collective-permute-start.27
  1278.1 27.9 %collective-permute-start.1 = (bf16[48,96,128]{2,1,0:T(8,128)(2,1)}, bf16[48,96,128]{2,1,0:T(8,128)(2,1)S(1)}, u32[]{:S(2)}, u32[]{:S(2)}) collective-permute-start(bf16[48,96,128]{2,1,0:T(8,128)(2,1)} %get-tuple-element.41), channel_id=1, source_target_pairs={{0,2},{1,3},{2,0},{3,1},{4,6},{5,7},{6,4},{7,5},{8,10},{9,11},{10,... | collective-permute-start | bytes 3538952 | tf_op jit(solution)/shard_map/ppermute | solution.py:611
  1278.2 52.9 %collective-permute-start.2 = (bf16[48,96,128]{2,1,0:T(8,128)(2,1)}, bf16[48,96,128]{2,1,0:T(8,128)(2,1)}, u32[]{:S(2)}, u32[]{:S(2)}) collective-permute-start(bf16[48,96,128]{2,1,0:T(8,128)(2,1)} %get-tuple-element.42), channel_id=1, source_target_pairs={{0,3},{1,0},{2,1},{3,2},{4,7},{5,4},{6,5},{7,6},{8,11},{9,8},{10,9... | collective-permute-start | bytes 3538952 | tf_op jit(solution)/shard_map/ppermute | solution.py:611
  1278.6 52.5 %collective-permute-start.17 = (bf16[48,96,128]{2,1,0:T(8,128)(2,1)}, bf16[48,96,128]{2,1,0:T(8,128)(2,1)}, u32[]{:S(2)}, u32[]{:S(2)}) collective-permute-start(bf16[48,96,128]{2,1,0:T(8,128)(2,1)} %get-tuple-element.56), channel_id=1, source_target_pairs={{0,1},{1,2},{2,3},{3,0},{4,5},{5,6},{6,7},{7,4},{8,9},{9,10},{10,1... | collective-permute-start | bytes 3538952 | tf_op jit(solution)/shard_map/ppermute | solution.py:611
  1280.0 76.7 %collective-permute-start.18 = (bf16[48,96,128]{2,1,0:T(8,128)(2,1)}, bf16[48,96,128]{2,1,0:T(8,128)(2,1)}, u32[]{:S(2)}, u32[]{:S(2)}) collective-permute-start(bf16[48,96,128]{2,1,0:T(8,128)(2,1)} %get-tuple-element.57), channel_id=1, source_target_pairs={{0,2},{1,3},{2,0},{3,1},{4,6},{5,7},{6,4},{7,5},{8,10},{9,11},{10,... | collective-permute-start | bytes 3538952 | tf_op jit(solution)/shard_map/ppermute | solution.py:611
  1281.4 87.6 %collective-permute-start.19 = (bf16[48,96,128]{2,1,0:T(8,128)(2,1)}, bf16[48,96,128]{2,1,0:T(8,128)(2,1)}, u32[]{:S(2)}, u32[]{:S(2)}) collective-permute-start(bf16[48,96,128]{2,1,0:T(8,128)(2,1)} %get-tuple-element.58), channel_id=1, source_target_pairs={{0,3},{1,0},{2,1},{3,2},{4,7},{5,4},{6,5},{7,6},{8,11},{9,8},{10,9... | collective-permute-start | bytes 3538952 | tf_op jit(solution)/shard_map/ppermute | solution.py:611
  (33 other events, 768.2 us)
Sparse Core Ops, SparseCore 0:
  253.9 25.5 reduce-scatter.1

commit v2 on v1

v2 whole, which is shorter than its diff:
```python
import functools
import math

import jax
import jax.numpy as jnp
from jax import lax
from jax.experimental import pallas as pl
from jax.experimental.pallas import tpu as pltpu
from jax.sharding import PartitionSpec as P

BF16 = jnp.bfloat16
F32 = jnp.float32
VMEM_BYTES = 56 * 1024 * 1024


def whole_spec(array):
    rank = array.ndim
    return pl.BlockSpec(array.shape, lambda *_: (0,) * rank)


def call(body, grid, in_specs, out_specs, out_shape, flops, moved, scratch=(), **extra):
    return pl.pallas_call(
        body,
        grid=grid,
        in_specs=in_specs,
        out_specs=out_specs,
        out_shape=out_shape,
        scratch_shapes=list(scratch),
        compiler_params=pltpu.CompilerParams(vmem_limit_bytes=VMEM_BYTES),
        cost_estimate=pl.CostEstimate(
            flops=int(flops), bytes_accessed=int(moved), transcendentals=0
        ),
        **extra,
    )


def dot(left, right):
    return jnp.dot(left, right, preferred_element_type=F32)


def tie(value, *others):
    others = jax.tree.leaves(others)
    anywhere = pl.BlockSpec(memory_space=pl.ANY)

    def body(*refs):
        pass

    return pl.pallas_call(
        body,
        in_specs=[anywhere] * (1 + len(others)),
        out_specs=anywhere,
        out_shape=jax.ShapeDtypeStruct(value.shape, value.dtype),
        input_output_aliases={0: 0},
        cost_estimate=pl.CostEstimate(flops=0, bytes_accessed=0, transcendentals=0),
    )(value, *others)


def cosine_tables(count):
    degree = jnp.arange(count, dtype=jnp.int32)
    points = jnp.arange(count, dtype=jnp.int32)
    phase = degree[None, :] * (2 * points[:, None] + 1) % (4 * count)
    basis = jnp.cos(phase.astype(F32) * (math.pi / (2 * count)))
    forward = (basis / count).astype(BF16)
    factor = jnp.where(degree == 0, 1.0, 2.0).astype(F32)
    inverse = (basis.T * factor[:, None]).astype(BF16)
    return (forward, inverse)


def shift_from(block, axis, step):
    count = lax.axis_size(axis)
    pairs = [(i, i + step) for i in range(count) if 0 <= i + step < count]
    return lax.ppermute(block, axis, pairs)


def halo_rows(block):
    return shift_from(block[:, -3:], "lat", 1), shift_from(block[:, :3], "lat", -1)


def halo_columns(block, top, bottom):
    def edge(span):
        return jnp.concatenate([piece[..., span] for piece in (top, block, bottom)], axis=1)

    left = shift_from(edge(slice(-3, None)), "chan", 1)
    right = shift_from(edge(slice(0, 3)), "chan", -1)
    return left, right


def turn_kernel(field_ref, out_ref):
    out_ref[...] = jnp.swapaxes(field_ref[0], 0, 1)


def turn(field, probe):
    rows, channels, lon_count = field.shape[1:]
    lanes = 128
    return call(
        turn_kernel,
        (lon_count // lanes,),
        [pl.BlockSpec((1, rows, channels, lanes), lambda x: (probe, 0, 0, x))],
        pl.BlockSpec((channels, rows, lanes), lambda x: (0, 0, x)),
        jax.ShapeDtypeStruct((channels, rows, lon_count), BF16),
        0,
        4 * rows * channels * lon_count,
    )(field)


def mix_kernel(fwd_ref, inv_ref, filter_ref, *refs):
    field_refs, out_ref = refs[:-1], refs[-1]
    lat_devices, channels, rows, width = field_refs[0].shape
    lon_blocks = len(field_refs)
    for channel in range(channels):
        block = jnp.concatenate([field_ref[:, channel] for field_ref in field_refs], axis=2)
        if rows % 16:
            block = block.astype(F32)
        field = block.reshape(lat_devices * rows, lon_blocks * width).astype(BF16)
        spectrum = dot(fwd_ref[...], field)
        filtered = (spectrum * filter_ref[channel]).astype(BF16)
        mixed = field.astype(F32) + dot(inv_ref[...], filtered)
        for band in range(lat_devices):
            for lon in range(lon_blocks):
                out_ref[band * lon_blocks + lon, channel] = mixed[
                    band * rows : (band + 1) * rows, lon * width : (lon + 1) * width
                ].astype(BF16)


def mix_latitudes(gathered, fwd_rows, inv_rows, filters, lon_blocks, part, parts):
    lat_devices, channels, rows, lanes = gathered.shape
    width = lanes // (lon_blocks * parts)
    count = lat_devices * rows
    peers = lat_devices * lon_blocks
    step = 2 if channels % 2 == 0 else 1

    def lines(lon):
        return pl.BlockSpec(
            (lat_devices, step, rows, width), lambda c: (0, c, 0, lon * parts + part)
        )

    return call(
        mix_kernel,
        (channels // step,),
        [
            whole_spec(fwd_rows),
            whole_spec(inv_rows),
            pl.BlockSpec((step, count, 1), lambda c: (c, 0, 0)),
        ]
        + [lines(lon) for lon in range(lon_blocks)],
        pl.BlockSpec((peers, step, rows, width), lambda c: (0, c, 0, 0)),
        jax.ShapeDtypeStruct((peers, channels, rows, width), BF16),
        4 * count * count * lanes * channels // parts,
        4 * gathered.size // parts,
    )(fwd_rows, inv_rows, filters, *([gathered] * lon_blocks))


def network_kernel(mixed_ref, slope_ref, win_ref, wout_ref, wflux_ref, flux_ref, *piece_refs):
    rows, _, lanes = mixed_ref.shape
    width = piece_refs[0].shape[1]
    together = max(1, 256 // lanes)
    for first in range(0, rows, together):
        span = range(first, first + together)
        mixed = jnp.concatenate([mixed_ref[row] for row in span], axis=1)
        slope = jnp.concatenate([slope_ref[row] for row in span], axis=1)
        hidden = dot(win_ref[...], mixed)
        gated = (slope.astype(F32) * hidden).astype(BF16)
        update = dot(wout_ref[...], gated).astype(BF16)
        flux = dot(wflux_ref[...], update)
        for place, row in enumerate(span):
            part = slice(place * lanes, (place + 1) * lanes)
            flux_ref[:, row] = flux[:, part]
            for index, piece_ref in enumerate(piece_refs):
                piece_ref[row] = update[index * width : (index + 1) * width, part]


def network(mixed, slope, part, win, wout, wflux, pieces):
    rows, channels, lanes = mixed.shape
    hidden = slope.shape[1]
    fluxes = wflux.shape[0]
    width = channels // pieces
    step = 8
    return call(
        network_kernel,
        (rows // step,),
        [
            pl.BlockSpec((step, channels, lanes), lambda n: (n, 0, 0)),
            pl.BlockSpec((step, hidden, lanes), lambda n: (n, 0, part)),
            whole_spec(win),
            whole_spec(wout),
            whole_spec(wflux),
        ],
        [pl.BlockSpec((fluxes, step, lanes), lambda n: (0, n, 0))]
        + [pl.BlockSpec((step, width, lanes), lambda n: (n, 0, 0))] * pieces,
        [jax.ShapeDtypeStruct((fluxes, rows, lanes), F32)]
        + [jax.ShapeDtypeStruct((rows, width, lanes), BF16)] * pieces,
        4 * rows * lanes * channels * hidden,
        2 * rows * lanes * (2 * channels + hidden),
    )(mixed, slope, win, wout, wflux)


def finish_kernel(columns, place_ref, field_ref, *refs):
    out_ref = refs[-1]
    for shift in range(columns):

        @pl.when(pl.program_id(1) == shift)
        def _(shift=shift):
            out_ref[0] = (field_ref[0].astype(F32) + refs[shift][...].astype(F32)).astype(BF16)


def finish(probe, part, parts, place, field, pieces, previous):
    rows, channels, lanes = pieces[0].shape
    columns = len(pieces)
    step = 16 if rows % 16 == 0 else 8

    def where(n, shift, place_ref):
        block = lax.rem(place_ref[0] - shift + columns, columns)
        return (probe, n, 0, block * parts + part)

    block = pl.BlockSpec((1, step, channels, lanes), where)
    piece = pl.BlockSpec((step, channels, lanes), lambda n, shift, place_ref: (n, 0, 0))
    operands = [place, field, *pieces]
    specs = [block] + [piece] * columns
    aliases = {}
    if previous is not None:
        aliases = {len(operands): 0}
        operands.append(previous)
        specs.append(pl.BlockSpec(memory_space=pl.ANY))
    return pl.pallas_call(
        functools.partial(finish_kernel, columns),
        grid_spec=pltpu.PrefetchScalarGridSpec(
            num_scalar_prefetch=1,
            grid=(rows // step, columns),
            in_specs=specs,
            out_specs=block,
        ),
        out_shape=jax.ShapeDtypeStruct(field.shape, BF16),
        input_output_aliases=aliases,
        compiler_params=pltpu.CompilerParams(vmem_limit_bytes=VMEM_BYTES),
        cost_estimate=pl.CostEstimate(
            flops=rows * channels * lanes * columns,
            bytes_accessed=6 * rows * channels * lanes * columns,
            transcendentals=0,
        ),
    )(*operands)


def pick_kernel(row_ref, col_ref, field_ref, *refs):
    part_refs, out_ref = refs[:-1], refs[-1]
    fields, rows, lanes = field_ref.shape
    cells = row_ref.shape[1]
    chosen = lax.broadcasted_iota(jnp.int32, (rows, cells), 0) == row_ref[...]
    chosen = jnp.where(chosen, 1.0, 0.0).astype(BF16)
    column = lax.broadcasted_iota(jnp.int32, (lanes, cells), 0) == col_ref[...]
    for field in range(fields):
        update = jnp.concatenate([part_ref[field] for part_ref in part_refs], axis=1)
        tile = (field_ref[field].astype(F32) + update).astype(BF16)
        lines = lax.dot_general(
            tile, chosen, (((0,), (0,)), ((), ())), preferred_element_type=F32
        )
        picked = jnp.sum(jnp.where(column, lines, 0.0), axis=0, keepdims=True).astype(BF16)
        count = out_ref.shape[2]
        for band in range(out_ref.shape[0]):
            out_ref[band, field : field + 1] = picked[
                :, band * count : (band + 1) * count
            ]


def pick_cells(row, col, field, parts, bands):
    cells = row.shape[1]
    fields = field.shape[0]
    operands = (row, col, field, *parts)
    return call(
        pick_kernel,
        (1,),
        [whole_spec(operand) for operand in operands],
        pl.BlockSpec((bands, fields, cells // bands), lambda _: (0, 0, 0)),
        jax.ShapeDtypeStruct((bands, fields, cells // bands), BF16),
        4 * field.size * cells,
        8 * field.size,
    )(*operands)


def regrid_kernel(slot_ref, weight_ref, high_ref, low_ref):
    slots = high_ref.shape[1]
    lanes = high_ref.shape[2]
    number = lax.broadcasted_iota(jnp.int32, (slots, lanes), 0)
    total = jnp.zeros((slots, lanes), F32)
    for source in range(slot_ref.shape[1]):
        total = total + jnp.where(
            number == slot_ref[0, source : source + 1], weight_ref[0, source : source + 1], 0.0
        )
    high = total.astype(BF16)
    high_ref[0] = high
    low_ref[0] = (total - high.astype(F32)).astype(BF16)


def regrid_matrix(slot, weight, slots):
    rows, sources, lanes = slot.shape
    line = pl.BlockSpec((1, sources, lanes), lambda y: (y, 0, 0))
    table = pl.BlockSpec((1, slots, lanes), lambda y: (y, 0, 0))
    shape = jax.ShapeDtypeStruct((rows, slots, lanes), BF16)
    return call(
        regrid_kernel,
        (rows,),
        [line, line],
        [table, table],
        [shape, shape],
        12 * rows * slots * lanes,
        4 * rows * slots * lanes,
    )(slot, weight)


def start_kernel(pool_ref, high_ref, low_ref, coupling_ref, probe_ref, mask_ref, out_ref):
    pool = jnp.concatenate([pool_ref[band] for band in range(pool_ref.shape[0])], axis=1)
    flux = dot(pool, high_ref[0]) + dot(pool, low_ref[0])
    coupling = coupling_ref[...]
    fields = coupling.shape[1]
    for probe in range(probe_ref.shape[0]):
        total = probe_ref[probe, 0].astype(F32)
        for field in range(fields):
            line = probe * fields + field
            total = total + coupling[:, field : field + 1] * flux[line : line + 1]
        out_ref[probe, 0] = (total * mask_ref[0]).astype(BF16)


def start_level(pool, high, low, coupling, probe, mask):
    probes, rows, channels, lanes = probe.shape
    slots = high.shape[1]
    table = pl.BlockSpec((1, slots, lanes), lambda y: (y, 0, 0))
    line = pl.BlockSpec((probes, 1, channels, lanes), lambda y: (0, y, 0, 0))
    return call(
        start_kernel,
        (rows,),
        [
            whole_spec(pool),
            table,
            table,
            whole_spec(coupling),
            line,
            pl.BlockSpec((1, 1, lanes), lambda y: (y, 0, 0)),
        ],
        line,
        jax.ShapeDtypeStruct(probe.shape, BF16),
        32 * high.size,
        4 * high.size,
    )(pool, high, low, coupling, probe, mask)


def fill_padded(padded_ref, field_ref, top_ref, bottom_ref, left_ref, right_ref):
    rows, channels, lanes = field_ref.shape[1:]
    empty = jnp.zeros((channels, 122), F32)
    for line in range(rows + 6):
        if line < 3:
            inner = top_ref[0, line]
        elif line < rows + 3:
            inner = field_ref[0, line - 3]
        else:
            inner = bottom_ref[0, line - rows - 3]
        padded_ref[line, :, :lanes] = inner.astype(F32)
        padded_ref[line, :, lanes:] = jnp.concatenate(
            [right_ref[0, line].astype(F32), empty, left_ref[0, line].astype(F32)], axis=1
        )


def spread_rows(padded_ref, taps_ref, spread_ref):
    rows, channels, lanes = spread_ref.shape
    tiles = padded_ref.shape[2] // 128

    def step(index, carry):
        span = pl.ds(pl.multiple_of(index * 8, 8), 8)
        taps = taps_ref[span, :]
        totals = [jnp.zeros((8, lanes), F32) for _ in range(rows)]
        for right in range(7):
            sums = [[None] * tiles for _ in range(rows)]
            weights = [
                jnp.broadcast_to(taps[:, down * 7 + right : down * 7 + right + 1], (8, 128))
                for down in range(7)
            ]
            for line in range(rows + 6):
                for tile in range(tiles):
                    value = padded_ref[line, span, tile * 128 : (tile + 1) * 128]
                    for down in range(7):
                        row = line - down
                        if 0 <= row < rows:
                            term = value * weights[down]
                            held = sums[row][tile]
                            sums[row][tile] = term if held is None else held + term
                row = line - 6
                if row >= 0:
                    whole = jnp.concatenate(sums[row], axis=1)
                    if right != 3:
                        whole = pltpu.roll(whole, (3 - right) % (tiles * 128), 1)
                    totals[row] = totals[row] + whole[:, :lanes]
        for row in range(rows):
            spread_ref[row, span, :] = totals[row]
        return carry

    lax.fori_loop(0, channels // 8, step, 0)


def tangent_row(spread, base, scale, count):
    center = jnp.sum(spread, axis=0, keepdims=True) / count
    along = jnp.sum(base * spread, axis=0, keepdims=True) / count
    return (scale * (spread - center - base * along)).astype(BF16)


def split_dot(left, right):
    high = right.astype(BF16)
    low = (right - high.astype(F32)).astype(BF16)
    return dot(left, high) + dot(left, low)


def fine_kernel(
    field_ref,
    top_ref,
    bottom_ref,
    left_ref,
    right_ref,
    taps_ref,
    base_ref,
    sigma_ref,
    slope_ref,
    gain_ref,
    expand_ref,
    shrink_ref,
    down_ref,
    pairs_ref,
    mask_ref,
    level_ref,
    coarse_ref,
    padded_ref,
    spread_ref,
):
    first = pl.program_id(1) * 2
    channels = field_ref.shape[2]

    @pl.when(pl.program_id(1) == 0)
    def _():
        fill_padded(padded_ref, field_ref, top_ref, bottom_ref, left_ref, right_ref)
        spread_rows(padded_ref, taps_ref, spread_ref)

    pooled = None
    for slot in range(2):
        tangent = tangent_row(
            spread_ref[first + slot],
            base_ref[slot].astype(F32),
            gain_ref[...] * sigma_ref[slot],
            channels,
        )
        hidden = dot(expand_ref[...], tangent)
        gated = (slope_ref[slot].astype(F32) * hidden).astype(BF16)
        output = dot(shrink_ref[...], gated)
        field = field_ref[0, first + slot].astype(F32)
        level = ((field + output) * mask_ref[slot]).astype(BF16)
        level_ref[0, slot] = level
        share = dot(level, pairs_ref[...])
        pooled = share if pooled is None else pooled + share
    coarse_ref[0, 0] = split_dot(down_ref[...], pooled).astype(BF16)


def fine_level(field, sides, taps, base, sigma, slope, gain, expand, shrink, down, pairs, mask):
    probes, rows, channels, lanes = field.shape
    hidden = slope.shape[1]
    wide = down.shape[0]

    def of_probe(array):
        return pl.BlockSpec((1, *array.shape[1:]), lambda p, y: (p, 0, 0, 0))

    line = pl.BlockSpec((2, channels, lanes), lambda p, y: (y, 0, 0))
    thin = pl.BlockSpec((2, 1, lanes), lambda p, y: (y, 0, 0))
    return call(
        fine_kernel,
        (probes, rows // 2),
        [of_probe(field)]
        + [of_probe(side) for side in sides]
        + [
            whole_spec(taps),
            line,
            thin,
            pl.BlockSpec((2, hidden, lanes), lambda p, y: (y, 0, 0)),
            whole_spec(gain),
            whole_spec(expand),
            whole_spec(shrink),
            whole_spec(down),
            whole_spec(pairs),
            thin,
        ],
        [
            pl.BlockSpec((1, 2, channels, lanes), lambda p, y: (p, y, 0, 0)),
            pl.BlockSpec((1, 1, wide, lanes // 2), lambda p, y: (p, y, 0, 0)),
        ],
        [
            jax.ShapeDtypeStruct(field.shape, BF16),
            jax.ShapeDtypeStruct((probes, rows // 2, wide, lanes // 2), BF16),
        ],
        8 * probes * rows * lanes * channels * hidden,
        4 * slope.size + 8 * field.size,
        scratch=[
            pltpu.VMEM((rows + 6, channels, lanes + 128), F32),
            pltpu.VMEM((rows, channels, lanes), F32),
        ],
    )(field, *sides, taps, base, sigma, slope, gain, expand, shrink, down, pairs, mask)


def coarse_kernel(
    count,
    field_ref,
    top_ref,
    bottom_ref,
    left_ref,
    right_ref,
    level_ref,
    taps_ref,
    base_ref,
    sigma_ref,
    slope_ref,
    gain_ref,
    expand_ref,
    shrink_ref,
    up_ref,
    copies_ref,
    mask_ref,
    out_ref,
    padded_ref,
    spread_ref,
):
    _, rows, _, lanes = field_ref.shape
    fill_padded(padded_ref, field_ref, top_ref, bottom_ref, left_ref, right_ref)
    spread_rows(padded_ref, taps_ref, spread_ref)
    tangent = jnp.concatenate(
        [
            tangent_row(
                spread_ref[row],
                base_ref[row].astype(F32),
                gain_ref[...] * sigma_ref[row],
                count,
            )
            for row in range(rows)
        ],
        axis=1,
    )
    hidden = dot(expand_ref[...], tangent)
    gated = jnp.concatenate(
        [
            (slope_ref[row].astype(F32) * hidden[:, row * lanes : (row + 1) * lanes]).astype(BF16)
            for row in range(rows)
        ],
        axis=1,
    )
    output = dot(shrink_ref[...], gated)
    for row in range(rows):
        level = (
            field_ref[0, row].astype(F32) + output[:, row * lanes : (row + 1) * lanes]
        ).astype(BF16)
        raised = dot(up_ref[...], level)
        high = raised.astype(BF16)
        low = (raised - high.astype(F32)).astype(BF16)
        wide = dot(high, copies_ref[...]) + dot(low, copies_ref[...])
        for half in range(2):
            line = 2 * row + half
            total = (level_ref[0, line].astype(F32) + wide) * mask_ref[line]
            out_ref[0, line] = total.astype(BF16)


def coarse_level(count, field, sides, level, *constants):
    def of_probe(array):
        return pl.BlockSpec((1, *array.shape[1:]), lambda p: (p, 0, 0, 0))

    by_probe = (field, *sides, level)
    slope = constants[3]
    _, rows, channels, lanes = field.shape
    return call(
        functools.partial(coarse_kernel, count),
        (field.shape[0],),
        [of_probe(operand) for operand in by_probe]
        + [whole_spec(operand) for operand in constants],
        of_probe(level),
        jax.ShapeDtypeStruct(level.shape, BF16),
        8 * field.size * slope.shape[1],
        2 * slope.size + 4 * level.size,
        scratch=[
            pltpu.VMEM((rows + 6, channels, lanes + 128), F32),
            pltpu.VMEM((rows, channels, lanes), F32),
        ],
    )(*by_probe, *constants)


def widen(array, dim, size):
    pads = [(0, 0)] * array.ndim
    pads[dim] = (0, size - array.shape[dim])
    return jnp.pad(array, pads)


def local(
    probe_field,
    gate_slope,
    spectral_filter,
    weight_in,
    weight_out,
    weight_flux,
    send_cells,
    recv_slots,
    recv_weights,
    ocean_probe,
    ocean_mask,
    coupling,
    base_fine,
    sigma_fine,
    slope_fine,
    gain_fine,
    kernel_fine,
    expand_fine,
    shrink_fine,
    down_proj,
    base_coarse,
    sigma_coarse,
    slope_coarse,
    gain_coarse,
    kernel_coarse,
    expand_coarse,
    shrink_coarse,
    up_proj,
):
    probes, rows, width, lon_count = probe_field.shape
    lat_devices = lax.axis_size("lat")
    columns = lax.axis_size("chan")
    lat_place = lax.axis_index("lat")
    place = lax.axis_index("chan")
    channels = width * columns
    group = width // lat_devices
    lon_block = lon_count // columns
    lanes = min(128, lon_block)
    parts = lon_block // lanes
    fluxes = weight_flux.shape[1]

    fwd_lat, inv_lat = cosine_tables(rows * lat_devices)
    fwd_rows, inv_rows = fwd_lat.T, inv_lat.T
    filters = lax.dynamic_slice_in_dim(spectral_filter, lat_place * group, group, 1).T[:, :, None]
    win = (
        weight_in.reshape(columns, lat_devices, group, -1)
        .transpose(3, 1, 0, 2)
        .reshape(-1, channels)
    )
    wout = jnp.roll(weight_out.T, -place * width, axis=0)
    wflux = jnp.roll(weight_flux.T, -place * width, axis=1)
    flux_rows = lax.dynamic_slice_in_dim(weight_flux, place * width, width, 0)

    flux_share = jnp.einsum(
        "pncx,cf->pfnx", probe_field, flux_rows, preferred_element_type=F32
    ).astype(BF16)
    flux_share = flux_share.reshape(probes * fluxes * rows, columns, lon_block).transpose(1, 0, 2)
    flux_field = lax.psum_scatter(flux_share, "chan", scatter_dimension=0, tiled=False)
    flux_field = flux_field.reshape(probes, fluxes, rows, lon_block)

    tile_rows, tile_cols = ocean_probe.shape[2:]
    slots = lat_devices * send_cells.shape[2]
    cells = send_cells.reshape(1, -1)
    cell_row, cell_col = cells // lon_block, cells % lon_block
    sources = recv_slots.shape[1]
    regrid_high, regrid_low = regrid_matrix(
        recv_slots.reshape(sources, tile_rows, tile_cols).transpose(1, 0, 2),
        recv_weights.reshape(sources, tile_rows, tile_cols).transpose(1, 0, 2),
        slots,
    )
    mask = ocean_mask.astype(F32)[:, None, :]
    ocean_start = ocean_probe.transpose(0, 2, 1, 3)
    coupling_rows = coupling.T.astype(F32)
    fine_count = kernel_fine.shape[0]
    coarse_count = kernel_coarse.shape[0]
    wide = -(-coarse_count // 64) * 64
    fine_args = (
        kernel_fine,
        base_fine.transpose(1, 0, 2),
        sigma_fine[:, None, :],
        slope_fine.transpose(1, 0, 2),
        gain_fine[:, None],
        expand_fine.T,
        shrink_fine.T,
        widen(down_proj.T, 0, wide),
    )
    column = jnp.arange(tile_cols)
    pairs = jnp.where(column[:, None] // 2 == jnp.arange(tile_cols // 2)[None, :], 0.25, 0.0)
    pairs = pairs.astype(BF16)
    copies = jnp.where(jnp.arange(tile_cols // 2)[:, None] == column[None, :] // 2, 1.0, 0.0)
    copies = copies.astype(BF16)
    coarse_args = (
        widen(kernel_coarse, 0, wide),
        widen(base_coarse.transpose(1, 0, 2), 1, wide),
        sigma_coarse[:, None, :],
        slope_coarse.transpose(1, 0, 2),
        widen(gain_coarse[:, None], 0, wide),
        widen(expand_coarse.T, 1, wide),
        widen(shrink_coarse.T, 0, wide),
        widen(up_proj.T, 1, wide),
        copies,
    )

    def exchange(block, axes):
        return lax.all_to_all(block, axes, split_axis=0, concat_axis=0, tiled=True)

    def send_update(mixed, part):
        mixed = mixed.reshape(channels, rows, -1).transpose(1, 0, 2)
        flux, *pieces = network(mixed, gate_slope, part, win, wout, wflux, columns)
        arrived = [pieces[0]]
        for shift in range(1, columns):
            pairs_of = [(source, (source + shift) % columns) for source in range(columns)]
            arrived.append(lax.ppermute(pieces[shift], "chan", pairs_of))
        return flux, arrived

    prepared = (
        flux_field,
        regrid_high,
        regrid_low,
        mask,
        ocean_start,
        coupling_rows,
        fine_args,
        coarse_args,
        pairs,
        win,
        wout,
        wflux,
        cell_row,
        cell_col,
    )
    parts_of = [1] * (probes - 1) + [parts]
    place_word = place.astype(jnp.int32).reshape(1)

    def gather(probe, *others):
        block = turn(probe_field, probe).reshape(lat_devices, group, rows, lon_count)
        return exchange(tie(block, *others) if others else block, "lat")

    def mix(probe, part, gathered):
        return mix_latitudes(
            gathered, fwd_rows, inv_rows, filters, columns, part, parts_of[probe]
        )

    def give_back(mixed, *others):
        return exchange(tie(mixed, *others), ("lat", "chan"))

    def pick(probe, updates):
        fluxes_of = [update[0] for update in updates]
        return pick_cells(cell_row, cell_col, flux_field[probe], fluxes_of, lat_devices)

    def begin(probe, pool):
        return start_level(
            pool,
            regrid_high,
            regrid_low,
            coupling_rows,
            ocean_start[probe : probe + 1],
            mask,
        )

    def fine(start, ends, *others):
        left, right = halo_columns(start, *ends)
        if others:
            left = tie(left, *others)
        return fine_level(start, (*ends, left, right), *fine_args, pairs, mask)

    def coarse(level, field, *others):
        ends = halo_rows(field)
        left, right = halo_columns(field, *ends)
        if others:
            left = tie(left, *others)
        sides = (*ends, left, right)
        out = coarse_level(coarse_count, field, sides, level, *coarse_args, mask)
        return out[0].transpose(1, 0, 2)

    def finish_all(probe, updates, atmos_out):
        for part, update in enumerate(updates):
            atmos_out = finish(
                probe, part, len(updates), place_word, probe_field, update[1], atmos_out
            )
        return atmos_out

    atmos_out = None
    gathered = gather(0)
    ahead = [prepared, flux_share]
    for probe in range(probes - 1):
        mixed = mix(probe, 0, gathered)
        arrived = give_back(mixed, gathered, ahead)
        gathered = gather(probe + 1, arrived)
        updates = [send_update(arrived, 0)]
        pool = lax.all_gather(pick(probe, updates), "lat", axis=0, tiled=False)
        pool = lax.dynamic_index_in_dim(pool, lat_place, 1, keepdims=False)
        start = begin(probe, pool)
        atmos_out = finish_all(probe, updates, atmos_out)
        ends = halo_rows(start)
        ahead = [ends, atmos_out]

    results = []
    probe = probes - 1
    arrived = [give_back(mix(probe, 0, gathered), gathered, ahead)]
    level, low = fine(start, ends)
    for part in range(1, parts):
        arrived.append(give_back(mix(probe, part, gathered), arrived[-1], low))
    updates = [send_update(arrived[part], part) for part in range(parts - 1)]
    before = [update[0] for update in updates]
    updates.append(send_update(tie(arrived[-1], before), parts - 1))
    pool = exchange(pick(probe, updates), "lat")
    results.append(coarse(level, tie(low, updates[-1][0])))
    back = [update[1] for update in updates[:-1]]
    start = begin(probe, tie(pool, back) if back else pool)
    level, low = fine(start, halo_rows(start))
    results.append(coarse(level, low, updates[-1][1], results[0]))
    atmos_out = finish_all(probe, updates, atmos_out)
    return (atmos_out, jnp.stack(results))


def solution(mesh):
    return jax.shard_map(
        local,
        mesh=mesh,
        in_specs=(
            P(None, "lat", "chan", None),
            P("lat", None, "chan"),
            P(None, "chan"),
            P(),
            P(),
            P(),
            P(("lat", "chan"), None, None),
            P(("lat", "chan"), None, None),
            P(("lat", "chan"), None, None),
            P(None, None, "lat", "chan"),
            P("lat", "chan"),
            P(),
            P(None, "lat", "chan"),
            P("lat", "chan"),
            P(None, "lat", "chan"),
            P(),
            P(),
            P(),
            P(),
            P(),
            P(None, "lat", "chan"),
            P("lat", "chan"),
            P(None, "lat", "chan"),
            P(),
            P(),
            P(),
            P(),
            P(),
        ),
        out_specs=(P(None, "lat", "chan", None), P(None, None, "lat", "chan")),
        check_vma=False,
    )
```

time: 1400 us -> 1170 us (0.84)
  waiting for transfers between devices: 722 us -> 482 us
  blocking collectives: 81.7 us -> 152 us
  local copies, waits for them, and re-layouts: 110 us -> 84.4 us
  other arithmetic: 26.6 us -> 12 us
    ppermute x12 -> x9, waiting for transfers between devices: 143 us -> 0.02 us  [send_update(): arrived.append(lax.ppermute(pieces[shift], 'chan', pairs_of))]
    all_gather x1, blocking collectives: 71.4 us -> 152 us  [local(): pool = lax.all_gather(pick(probe, updates), 'lat', axis=0, tiled=False)]
    ppermute x16, waiting for transfers between devices: 107 us -> 28 us  [shift_from(): return lax.ppermute(block, axis, pairs)]
    pallas_call x4 -> x3, Pallas kernels: 142 us -> 92.5 us  [network(): call(network_kernel, (rows // step,), [pl.BlockSpec((step, channels, lane...]
    pallas_call x8 -> x12, Pallas kernels: 131 us -> 170 us  [the longest x2 48.1 us: fine_level(): call(fine_kernel, (probes, rows // 2), [of_probe(field)] + [of_probe(side...]
    transpose x4 -> x1, local copies, waits for them, and re-layouts: 40.3 us -> 2.25 us  [coarse(): return out[0].transpose(1, 0, 2)]
    all_to_all x6, waiting for transfers between devices: 472 us -> 454 us  [exchange(): return lax.all_to_all(block, axes, split_axis=0, concat_axis=0, tiled=True)]
    ppermute x16, starting transfers between devices: 67.6 us -> 51.4 us  [shift_from(): return lax.ppermute(block, axis, pairs)]
  transfers between devices with their start and end apart: 35 -> 32, of which waited for: 21 -> 8; matrix products, arithmetic and copies ran while one was open for 7% -> 8% of each run, Pallas kernels for 17% -> 22%
where the time goes in v2:
time: 1170 us; the launch traced here: 1160 us
  waiting for transfers between devices  482 us (41%)
  Pallas kernels  290 us (25%)
  blocking collectives  152 us (13%)
  starting transfers between devices  113 us (10%)
  local copies, waits for them, and re-layouts  84.4 us (7%)
  between operations  15.2 us (1%)
  other arithmetic  12 us (1%)
    all_to_all x6, waiting for transfers between devices, exchange(): return lax.all_to_all(block, axes, split_axis=0, concat_axis=0, tiled=True)  454 us
    all_gather x1, blocking collectives, local(): pool = lax.all_gather(pick(probe, updates), 'lat', axis=0, tiled=False)  152 us
    pallas_call x3, Pallas kernels, network(): call(network_kernel, (rows // step,), [pl.BlockSpec((step, channels, lane...  92.5 us
    ppermute x16, starting transfers between devices, shift_from(): return lax.ppermute(block, axis, pairs)  51.4 us
    all_to_all x6, starting transfers between devices, exchange(): return lax.all_to_all(block, axes, split_axis=0, concat_axis=0, tiled=True)  51.2 us
    pallas_call x2, Pallas kernels, fine_level(): call(fine_kernel, (probes, rows // 2), [of_probe(field)] + [of_probe(side...  48.1 us
    pallas_call x3, Pallas kernels, finish(): pl.pallas_call(functools.partial(finish_kernel, columns), grid_spec=pltpu...  36.9 us
    pallas_call x3, Pallas kernels, mix_latitudes(): call(mix_kernel, (channels // step,), [whole_spec(fwd_rows), whole_spec(i...  35.3 us
  transfers between devices with their start and end apart: 32, of which 8 were waited for; matrix products, arithmetic and copies ran while one was open for 8% of the time, Pallas kernels for 22%

profile of v2, /device:TPU:9, one launch (start us, length us, event | category | flops | bytes accessed | tf_op | source)
XLA Modules:
  0.0 1156.7 jit_solution(855720178001227245)
XLA Ops:
  7.2 10.3 shard_map.276
  23.3 7.8 fusion
  58.7 7.1 shard_map.278
  76.3 150.9 %all-to-all-done.refs_0_.refs_1_.refs_2_.refs_3_ = bf16[8,12,48,1024]{3,2,1,0:T(8,128)(2,1)} async-done(((bf16[8,12,48,1024]{3,2,1,0:T(8,128)(2,1)}), bf16[8,12,48,1024]{3,2,1,0:T(8,128)(2,1)}, u32[]{:S(2)}, u32[]{:S(2)}) %all-to-all-start) | async-done | bytes 9437216 | tf_op jit(solution)/shard_map/all_to_all | solution.py:695
  227.1 14.3 %shard_map.277.refs_0_ = bf16[32,12,48,256]{3,2,1,0:T(8,128)(2,1)} custom-call(bf16[384,384]{1,0:T(8,128)(2,1)} %get-tuple-element.89.fwd_ref, bf16[384,384]{1,0:T(8,128)(2,1)} %get-tuple-element.88.inv_ref, f32[12,384,1]{2,1,0:T(8,128)} %copy.114.filter_ref, bf16[8,12,48,1024]{3,2,1,0:T(8,128)(2,1)} %all-to-all-done.refs_0_.refs_1_.refs_2_.refs_3_, ...), custom_call_target="tpu_custom_call" | custom-call | flops 7247757312 | bytes 18874368 | tf_op jit(solution)/shard_map/pallas_call | solution.py:137
  241.5 6.2 all-to-all-start.1
  247.7 10.5 shard_map.275
  258.1 192.7 %all-to-all-done.1.refs_1_ = bf16[32,12,48,256]{3,2,1,0:T(8,128)(2,1)} async-done(((bf16[32,12,48,256]{3,2,1,0:T(8,128)(2,1)}), bf16[32,12,48,256]{3,2,1,0:T(8,128)(2,1)}, u32[]{:S(2)}, u32[]{:S(2)}) %all-to-all-start.1) | async-done | bytes 9437216 | tf_op jit(solution)/shard_map/all_to_all | solution.py:695
  450.9 9.6 all-to-all-start.2
  460.5 10.8 copy.172
  471.3 45.1 %shard_map.283 = (f32[4,48,256]{2,1,0:T(8,128)}, bf16[48,96,256]{2,1,0:T(8,128)(2,1)}, bf16[48,96,256]{2,1,0:T(8,128)(2,1)}, bf16[48,96,256]{2,1,0:T(8,128)(2,1)}, bf16[48,96,256]{2,1,0:T(8,128)(2,1)}) custom-call(bf16[48,384,256]{2,1,0:T(8,128)(2,1)} %bitcast.97, bf16[48,768,256]{2,1,0:T(8,128)(2,1)} %slope_ref.5, bf16[768,384]{1,0:T(8,128)(2,1)} %copy.113.refs_26_.win_ref, ...), custom_call_target="tpu_custom_call" | custom-call | flops 14495514624 | bytes 37748736 | tf_op jit(solution)/shard_map/pallas_call | solution.py:178
  526.6 151.8 %all-gather = bf16[64,4,128]{2,1,0:T(4,128)(2,1)S(1)} all-gather(bf16[8,4,128]{2,1,0:T(4,128)(2,1)} %shard_map.284), channel_id=2, replica_groups=mesh['lat'=8,'chan'=4] {'lat'}, dimensions={0}, use_global_device_ids=true | all-gather | bytes 73728 | tf_op jit(solution)/shard_map/all_gather | solution.py:781
  679.1 8.1 shard_map.285.field_ref
  694.5 15.1 %shard_map.286.refs_4_ = bf16[2,48,96,1024]{3,2,1,0:T(8,128)(2,1)} custom-call(s32[1]{0:T(128)} %bitcast.place_ref, bf16[2,48,96,1024]{3,2,1,0:T(8,128)(2,1)} %field_ref.9, bf16[48,96,256]{2,1,0:T(8,128)(2,1)} %get-tuple-element.26.refs_0_, bf16[48,96,256]{2,1,0:T(8,128)(2,1)} %collective-permute-done.2.refs_1_, ...), custom_call_target="tpu_custom_call" | custom-call | flops 4718592 | bytes 28311552 | tf_op jit(solution)/shard_map/pallas_call | solution.py:224
  709.6 10.5 shard_map.282.refs_0_
  721.5 14.9 %all-to-all-start.3 = ((bf16[32,12,48,128]{3,2,1,0:T(8,128)(2,1)}), bf16[32,12,48,128]{3,2,1,0:T(8,128)(2,1)}, u32[]{:S(2)}, u32[]{:S(2)}) async-start(bf16[32,12,48,128]{3,2,1,0:T(8,128)(2,1)} %shard_map.287), calls=%async_computation.4 | async-start | bytes 9437184 | tf_op jit(solution)/shard_map/all_to_all | solution.py:695
  743.8 17.1 %collective-permute-done.5 = bf16[1,14,200,3]{2,1,3,0:T(8,128)(2,1)S(1)} collective-permute-done((bf16[1,14,200,3]{2,1,3,0:T(8,128)(2,1)S(1)}, bf16[1,14,200,3]{2,1,3,0:T(8,128)(2,1)S(1)}, u32[]{:S(2)}, u32[]{:S(2)}) %collective-permute-start.5) | collective-permute-done | bytes 16832 | tf_op jit(solution)/shard_map/ppermute | solution.py:72
  764.9 24.0 %shard_map.288 = (bf16[1,8,200,256]{3,2,1,0:T(8,128)(2,1)}, bf16[1,4,256,128]{3,2,1,0:T(8,128)(2,1)}) custom-call(bf16[1,8,200,256]{3,2,1,0:T(8,128)(2,1)} %shard_map.285.field_ref, bf16[1,3,200,256]{3,2,1,0:T(8,128)(2,1)} %copy-done.14, bf16[1,3,200,256]{3,2,1,0:T(8,128)(2,1)} %copy-done.16, bf16[1,14,200,3]{3,2,1,0:T(8,128)(2,1)} %copy.125.left_ref, ...), custom_call_target="tpu_custom_call" | custom-call | flops 2621440000 | bytes 9830400 | tf_op jit(solution)/shard_map/pallas_call | solution.py:467
  788.9 10.5 shard_map.281.refs_0_
  799.4 39.3 %all-to-all-done.3.refs_1_ = bf16[32,12,48,128]{3,2,1,0:T(8,128)(2,1)} async-done(((bf16[32,12,48,128]{3,2,1,0:T(8,128)(2,1)}), bf16[32,12,48,128]{3,2,1,0:T(8,128)(2,1)}, u32[]{:S(2)}, u32[]{:S(2)}) %all-to-all-start.3) | async-done | bytes 4718624 | tf_op jit(solution)/shard_map/all_to_all | solution.py:695
  838.7 8.6 all-to-all-start.4
  853.1 23.7 %shard_map.290 = (f32[4,48,128]{2,1,0:T(8,128)}, bf16[48,96,128]{2,1,0:T(8,128)(2,1)}, bf16[48,96,128]{2,1,0:T(8,128)(2,1)}, bf16[48,96,128]{2,1,0:T(8,128)(2,1)}, bf16[48,96,128]{2,1,0:T(8,128)(2,1)}) custom-call(bf16[48,384,128]{2,1,0:T(8,128)(2,1)} %bitcast.103, bf16[48,768,256]{2,1,0:T(8,128)(2,1)} %slope_ref.5, ...), custom_call_target="tpu_custom_call" | custom-call | flops 7247757312 | bytes 18874368 | tf_op jit(solution)/shard_map/pallas_call | solution.py:178
  878.8 71.0 %all-to-all-done.4.refs_0_ = bf16[32,12,48,128]{3,2,1,0:T(8,128)(2,1)} async-done(((bf16[32,12,48,128]{3,2,1,0:T(8,128)(2,1)}), bf16[32,12,48,128]{3,2,1,0:T(8,128)(2,1)}, u32[]{:S(2)}, u32[]{:S(2)}) %all-to-all-start.4) | async-done | bytes 4718624 | tf_op jit(solution)/shard_map/all_to_all | solution.py:695
  955.6 23.7 %shard_map.292 = (f32[4,48,128]{2,1,0:T(8,128)}, bf16[48,96,128]{2,1,0:T(8,128)(2,1)}, bf16[48,96,128]{2,1,0:T(8,128)(2,1)}, bf16[48,96,128]{2,1,0:T(8,128)(2,1)}, bf16[48,96,128]{2,1,0:T(8,128)(2,1)}) custom-call(bf16[48,384,128]{2,1,0:T(8,128)(2,1)} %bitcast.102, bf16[48,768,256]{2,1,0:T(8,128)(2,1)} %slope_ref.5, ...), custom_call_target="tpu_custom_call" | custom-call | flops 7247757312 | bytes 18874368 | tf_op jit(solution)/shard_map/pallas_call | solution.py:178
  999.0 8.1 shard_map.299.field_ref
  1016.7 6.9 collective-permute-start.15
  1036.8 10.9 shard_map.293.refs_4_
  1055.2 24.0 %shard_map.300 = (bf16[1,8,200,256]{3,2,1,0:T(8,128)(2,1)}, bf16[1,4,256,128]{3,2,1,0:T(8,128)(2,1)}) custom-call(bf16[1,8,200,256]{3,2,1,0:T(8,128)(2,1)} %shard_map.299.field_ref, bf16[1,3,200,256]{3,2,1,0:T(8,128)(2,1)} %copy-done.24, bf16[1,3,200,256]{3,2,1,0:T(8,128)(2,1)} %copy-done.25, bf16[1,14,200,3]{3,2,1,0:T(8,128)(2,1)} %copy.147.left_ref, ...), custom_call_target="tpu_custom_call" | custom-call | flops 2621440000 | bytes 9830400 | tf_op jit(solution)/shard_map/pallas_call | solution.py:467
  1088.8 6.4 collective-permute-done.22.bottom_ref
  1101.1 14.3 %shard_map.296 = bf16[1,8,200,256]{3,2,1,0:T(8,128)(2,1)} custom-call(bf16[1,4,256,128]{3,2,1,0:T(8,128)(2,1)} %shard_map.295.field_ref, bf16[1,3,256,128]{3,2,1,0:T(8,128)(2,1)} %copy-done.10, bf16[1,3,256,128]{3,2,1,0:T(8,128)(2,1)} %copy-done.11, bf16[1,10,256,3]{3,2,1,0:T(8,128)(2,1)} %copy.139.left_ref, bf16[1,10,256,3]{3,2,1,0:T(8,128)(2,1)} %copy.140.right_ref, ...), custom_call_target="tpu_custom_call" | custom-call | flops 1048576000 | bytes 2662400 | tf_op jit(solution)/shard_map/pallas_call | solution.py:568
  1121.4 14.3 %shard_map.302 = bf16[1,8,200,256]{3,2,1,0:T(8,128)(2,1)} custom-call(bf16[1,4,256,128]{3,2,1,0:T(8,128)(2,1)} %get-tuple-element.42.field_ref, bf16[1,3,256,128]{3,2,1,0:T(8,128)(2,1)} %copy-done.12, bf16[1,3,256,128]{3,2,1,0:T(8,128)(2,1)} %copy-done.13, bf16[1,10,256,3]{3,2,1,0:T(8,128)(2,1)} %shard_map.301.left_ref, ...), custom_call_target="tpu_custom_call" | custom-call | flops 1048576000 | bytes 2662400 | tf_op jit(solution)/shard_map/pallas_call | solution.py:568
  1138.5 10.9 shard_map.294
  (245 shorter events, 162.1 us)
Async XLA Ops:
  17.5 209.6 %all-to-all-start = ((bf16[8,12,48,1024]{3,2,1,0:T(8,128)(2,1)}), bf16[8,12,48,1024]{3,2,1,0:T(8,128)(2,1)}, u32[]{:S(2)}, u32[]{:S(2)}) async-start(bf16[8,12,48,1024]{3,2,1,0:T(8,128)(2,1)} %bitcast.88), calls=%async_computation | async-start | bytes 18874368 | tf_op jit(solution)/shard_map/all_to_all | solution.py:695
  23.3 218.1 %reduce-scatter.2.cloned.1.call-start = ((), (), s32[]{:S(2)}) async-start(), calls=%async_computation.7 | async-start | bytes 983040 | tf_op jit(solution)/shard_map/reduce_scatter | solution.py:648
  241.5 209.4 %all-to-all-start.1 = ((bf16[32,12,48,256]{3,2,1,0:T(8,128)(2,1)}), bf16[32,12,48,256]{3,2,1,0:T(8,128)(2,1)}, u32[]{:S(2)}, u32[]{:S(2)}) async-start(bf16[32,12,48,256]{3,2,1,0:T(8,128)(2,1)} %shard_map.279), calls=%async_computation.2 | async-start | bytes 18874368 | tf_op jit(solution)/shard_map/all_to_all | solution.py:695
  450.9 258.7 %all-to-all-start.2 = ((bf16[8,12,48,1024]{3,2,1,0:T(8,128)(2,1)}), bf16[8,12,48,1024]{3,2,1,0:T(8,128)(2,1)}, u32[]{:S(2)}, u32[]{:S(2)}) async-start(bf16[8,12,48,1024]{3,2,1,0:T(8,128)(2,1)} %shard_map.280), calls=%async_computation.3 | async-start | bytes 18874368 | tf_op jit(solution)/shard_map/all_to_all | solution.py:695
  516.4 178.1 %collective-permute-start.2 = (bf16[48,96,256]{2,1,0:T(8,128)(2,1)}, bf16[48,96,256]{2,1,0:T(8,128)(2,1)}, u32[]{:S(2)}, u32[]{:S(2)}) collective-permute-start(bf16[48,96,256]{2,1,0:T(8,128)(2,1)} %get-tuple-element.27), channel_id=1, source_target_pairs={{0,1},{1,2},{2,3},{3,0},{4,5},{5,6},{6,7},{7,4},{8,9},{9,10},{10,1... | collective-permute-start | bytes 7077896 | tf_op jit(solution)/shard_map/ppermute | solution.py:703
  521.8 172.6 %collective-permute-start.3 = (bf16[48,96,256]{2,1,0:T(8,128)(2,1)}, bf16[48,96,256]{2,1,0:T(8,128)(2,1)}, u32[]{:S(2)}, u32[]{:S(2)}) collective-permute-start(bf16[48,96,256]{2,1,0:T(8,128)(2,1)} %get-tuple-element.28), channel_id=1, source_target_pairs={{0,2},{1,3},{2,0},{3,1},{4,6},{5,7},{6,4},{7,5},{8,10},{9,11},{10,... | collective-permute-start | bytes 7077896 | tf_op jit(solution)/shard_map/ppermute | solution.py:703
  521.8 172.7 %collective-permute-start.4 = (bf16[48,96,256]{2,1,0:T(8,128)(2,1)}, bf16[48,96,256]{2,1,0:T(8,128)(2,1)}, u32[]{:S(2)}, u32[]{:S(2)}) collective-permute-start(bf16[48,96,256]{2,1,0:T(8,128)(2,1)} %get-tuple-element.29), channel_id=1, source_target_pairs={{0,3},{1,0},{2,1},{3,2},{4,7},{5,4},{6,5},{7,6},{8,11},{9,8},{10,9... | collective-permute-start | bytes 7077896 | tf_op jit(solution)/shard_map/ppermute | solution.py:703
  688.2 31.8 %collective-permute-start = (bf16[1,3,200,256]{3,2,1,0:T(8,128)(2,1)S(1)}, bf16[1,3,200,256]{3,2,1,0:T(8,128)(2,1)S(1)}, u32[]{:S(2)}, u32[]{:S(2)}) collective-permute-start(bf16[1,3,200,256]{3,2,1,0:T(8,128)(2,1)S(1)} %get-tuple-element.61), channel_id=1, source_target_pairs={{0,4},{4,8},{8,12},{12,16},{16,20},{20,24},{24,28},{1,5},{5,9},{9,... | collective-permute-start | bytes 921608 | tf_op jit(solution)/shard_map/ppermute | solution.py:72
  690.2 29.9 %collective-permute-start.1 = (bf16[1,3,200,256]{3,2,1,0:T(8,128)(2,1)S(1)}, bf16[1,3,200,256]{3,2,1,0:T(8,128)(2,1)S(1)}, u32[]{:S(2)}, u32[]{:S(2)}) collective-permute-start(bf16[1,3,200,256]{3,2,1,0:T(8,128)(2,1)S(1)} %get-tuple-element.60), channel_id=1, source_target_pairs={{4,0},{8,4},{12,8},{16,12},{20,16},{24,20},{28,24},{5,1},{9,5},{13... | collective-permute-start | bytes 921608 | tf_op jit(solution)/shard_map/ppermute | solution.py:72
  721.5 117.2 %all-to-all-start.3 = ((bf16[32,12,48,128]{3,2,1,0:T(8,128)(2,1)}), bf16[32,12,48,128]{3,2,1,0:T(8,128)(2,1)}, u32[]{:S(2)}, u32[]{:S(2)}) async-start(bf16[32,12,48,128]{3,2,1,0:T(8,128)(2,1)} %shard_map.287), calls=%async_computation.4 | async-start | bytes 9437184 | tf_op jit(solution)/shard_map/all_to_all | solution.py:695
  738.0 22.8 %collective-permute-start.5 = (bf16[1,14,200,3]{2,1,3,0:T(8,128)(2,1)S(1)}, bf16[1,14,200,3]{2,1,3,0:T(8,128)(2,1)S(1)}, u32[]{:S(2)}, u32[]{:S(2)}) collective-permute-start(bf16[1,14,200,3]{2,1,3,0:T(8,128)(2,1)S(1)} %pad_maximum_fusion.1), channel_id=1, source_target_pairs={{0,1},{1,2},{2,3},{4,5},{5,6},{6,7},{8,9},{9,10},{10,11},{12,13},{... | collective-permute-start | bytes 50408 | tf_op jit(solution)/shard_map/ppermute | solution.py:72
  741.8 21.9 %collective-permute-start.6 = (bf16[1,14,200,3]{2,1,3,0:T(8,128)(2,1)S(1)}, bf16[1,14,200,3]{2,1,3,0:T(8,128)(2,1)S(1)}, u32[]{:S(2)}, u32[]{:S(2)}) collective-permute-start(bf16[1,14,200,3]{2,1,3,0:T(8,128)(2,1)S(1)} %pad_maximum_fusion.2), channel_id=1, source_target_pairs={{1,0},{2,1},{3,2},{5,4},{6,5},{7,6},{9,8},{10,9},{11,10},{13,12},{... | collective-permute-start | bytes 50408 | tf_op jit(solution)/shard_map/ppermute | solution.py:72
  838.7 111.1 %all-to-all-start.4 = ((bf16[32,12,48,128]{3,2,1,0:T(8,128)(2,1)}), bf16[32,12,48,128]{3,2,1,0:T(8,128)(2,1)}, u32[]{:S(2)}, u32[]{:S(2)}) async-start(bf16[32,12,48,128]{3,2,1,0:T(8,128)(2,1)} %shard_map.289), calls=%async_computation.5 | async-start | bytes 9437184 | tf_op jit(solution)/shard_map/all_to_all | solution.py:695
  876.8 120.8 %collective-permute-start.10 = (bf16[48,96,128]{2,1,0:T(8,128)(2,1)}, bf16[48,96,128]{2,1,0:T(8,128)(2,1)S(1)}, u32[]{:S(2)}, u32[]{:S(2)}) collective-permute-start(bf16[48,96,128]{2,1,0:T(8,128)(2,1)} %get-tuple-element.37), channel_id=1, source_target_pairs={{0,1},{1,2},{2,3},{3,0},{4,5},{5,6},{6,7},{7,4},{8,9},{9,10},{10,1... | collective-permute-start | bytes 3538952 | tf_op jit(solution)/shard_map/ppermute | solution.py:703
  878.3 119.3 %collective-permute-start.11 = (bf16[48,96,128]{2,1,0:T(8,128)(2,1)}, bf16[48,96,128]{2,1,0:T(8,128)(2,1)S(1)}, u32[]{:S(2)}, u32[]{:S(2)}) collective-permute-start(bf16[48,96,128]{2,1,0:T(8,128)(2,1)} %get-tuple-element.38), channel_id=1, source_target_pairs={{0,2},{1,3},{2,0},{3,1},{4,6},{5,7},{6,4},{7,5},{8,10},{9,11},{10,... | collective-permute-start | bytes 3538952 | tf_op jit(solution)/shard_map/ppermute | solution.py:703
  878.6 119.0 %collective-permute-start.12 = (bf16[48,96,128]{2,1,0:T(8,128)(2,1)}, bf16[48,96,128]{2,1,0:T(8,128)(2,1)}, u32[]{:S(2)}, u32[]{:S(2)}) collective-permute-start(bf16[48,96,128]{2,1,0:T(8,128)(2,1)} %get-tuple-element.39), channel_id=1, source_target_pairs={{0,3},{1,0},{2,1},{3,2},{4,7},{5,4},{6,5},{7,6},{8,11},{9,8},{10,9... | collective-permute-start | bytes 3538952 | tf_op jit(solution)/shard_map/ppermute | solution.py:703
  981.7 15.8 %all-to-all-start.5 = ((bf16[8,4,128]{2,1,0:T(4,128)(2,1)}), bf16[8,4,128]{2,1,0:T(4,128)(2,1)S(1)}, u32[]{:S(2)}, u32[]{:S(2)}) async-start(bf16[8,4,128]{2,1,0:T(4,128)(2,1)} %shard_map.297), calls=%async_computation.6 | async-start | bytes 16384 | tf_op jit(solution)/shard_map/all_to_all | solution.py:695
  990.8 25.6 %collective-permute-start.13 = (bf16[1,3,256,128]{3,2,1,0:T(8,128)(2,1)}, bf16[1,3,256,128]{3,2,1,0:T(8,128)(2,1)S(1)}, u32[]{:S(2)}, u32[]{:S(2)}) collective-permute-start(bf16[1,3,256,128]{3,2,1,0:T(8,128)(2,1)} %get-tuple-element.75), channel_id=1, source_target_pairs={{0,4},{4,8},{8,12},{12,16},{16,20},{20,24},{24,28},{1,5},{5,9},{9,... | collective-permute-start | bytes 589832 | tf_op jit(solution)/shard_map/ppermute | solution.py:72
  993.9 22.2 %collective-permute-start.14 = (bf16[1,3,256,128]{3,2,1,0:T(8,128)(2,1)}, bf16[1,3,256,128]{3,2,1,0:T(8,128)(2,1)S(1)}, u32[]{:S(2)}, u32[]{:S(2)}) collective-permute-start(bf16[1,3,256,128]{3,2,1,0:T(8,128)(2,1)} %get-tuple-element.74), channel_id=1, source_target_pairs={{4,0},{8,4},{12,8},{16,12},{20,16},{24,20},{28,24},{5,1},{9,5},{13... | collective-permute-start | bytes 589832 | tf_op jit(solution)/shard_map/ppermute | solution.py:72
  1008.2 18.8 %collective-permute-start.17 = (bf16[1,3,200,256]{3,2,1,0:T(8,128)(2,1)S(1)}, bf16[1,3,200,256]{3,2,1,0:T(8,128)(2,1)S(1)}, u32[]{:S(2)}, u32[]{:S(2)}) collective-permute-start(bf16[1,3,200,256]{3,2,1,0:T(8,128)(2,1)S(1)} %get-tuple-element.57), channel_id=1, source_target_pairs={{0,4},{4,8},{8,12},{12,16},{16,20},{20,24},{24,28},{1,5},{5,9},{9,... | collective-permute-start | bytes 921608 | tf_op jit(solution)/shard_map/ppermute | solution.py:72
  1010.4 16.4 %collective-permute-start.18 = (bf16[1,3,200,256]{3,2,1,0:T(8,128)(2,1)S(1)}, bf16[1,3,200,256]{3,2,1,0:T(8,128)(2,1)S(1)}, u32[]{:S(2)}, u32[]{:S(2)}) collective-permute-start(bf16[1,3,200,256]{3,2,1,0:T(8,128)(2,1)S(1)} %get-tuple-element.56), channel_id=1, source_target_pairs={{4,0},{8,4},{12,8},{16,12},{20,16},{24,20},{28,24},{5,1},{9,5},{13... | collective-permute-start | bytes 921608 | tf_op jit(solution)/shard_map/ppermute | solution.py:72
  1016.7 32.8 %collective-permute-start.15 = (bf16[1,10,256,3]{2,3,1,0:T(4,128)(2,1)S(1)}, bf16[1,10,256,3]{2,3,1,0:T(4,128)(2,1)S(1)}, u32[]{:S(2)}, u32[]{:S(2)}) collective-permute-start(bf16[1,10,256,3]{2,3,1,0:T(4,128)(2,1)S(1)} %pad_maximum_fusion.5), channel_id=1, source_target_pairs={{0,1},{1,2},{2,3},{4,5},{5,6},{6,7},{8,9},{9,10},{10,11},{12,13},{... | collective-permute-start | bytes 46088 | tf_op jit(solution)/shard_map/ppermute | solution.py:72
  1027.3 25.5 %collective-permute-start.19 = (bf16[1,14,200,3]{2,1,3,0:T(8,128)(2,1)S(1)}, bf16[1,14,200,3]{2,1,3,0:T(8,128)(2,1)S(1)}, u32[]{:S(2)}, u32[]{:S(2)}) collective-permute-start(bf16[1,14,200,3]{2,1,3,0:T(8,128)(2,1)S(1)} %pad_maximum_fusion.3), channel_id=1, source_target_pairs={{0,1},{1,2},{2,3},{4,5},{5,6},{6,7},{8,9},{9,10},{10,11},{12,13},{... | collective-permute-start | bytes 50408 | tf_op jit(solution)/shard_map/ppermute | solution.py:72
  1033.0 21.0 %collective-permute-start.20 = (bf16[1,14,200,3]{2,1,3,0:T(8,128)(2,1)S(1)}, bf16[1,14,200,3]{2,1,3,0:T(8,128)(2,1)S(1)}, u32[]{:S(2)}, u32[]{:S(2)}) collective-permute-start(bf16[1,14,200,3]{2,1,3,0:T(8,128)(2,1)S(1)} %pad_maximum_fusion.4), channel_id=1, source_target_pairs={{1,0},{2,1},{3,2},{5,4},{6,5},{7,6},{9,8},{10,9},{11,10},{13,12},{... | collective-permute-start | bytes 50408 | tf_op jit(solution)/shard_map/ppermute | solution.py:72
  1034.9 16.0 %collective-permute-start.16 = (bf16[1,10,256,3]{2,3,1,0:T(4,128)(2,1)S(1)}, bf16[1,10,256,3]{2,3,1,0:T(4,128)(2,1)S(1)}, u32[]{:S(2)}, u32[]{:S(2)}) collective-permute-start(bf16[1,10,256,3]{2,3,1,0:T(4,128)(2,1)S(1)} %pad_maximum_fusion.6), channel_id=1, source_target_pairs={{1,0},{2,1},{3,2},{5,4},{6,5},{7,6},{9,8},{10,9},{11,10},{13,12},{... | collective-permute-start | bytes 46088 | tf_op jit(solution)/shard_map/ppermute | solution.py:72
  1047.8 72.2 %collective-permute-start.7 = (bf16[48,96,128]{2,1,0:T(8,128)(2,1)}, bf16[48,96,128]{2,1,0:T(8,128)(2,1)S(1)}, u32[]{:S(2)}, u32[]{:S(2)}) collective-permute-start(bf16[48,96,128]{2,1,0:T(8,128)(2,1)} %get-tuple-element.33), channel_id=1, source_target_pairs={{0,1},{1,2},{2,3},{3,0},{4,5},{5,6},{6,7},{7,4},{8,9},{9,10},{10,1... | collective-permute-start | bytes 3538952 | tf_op jit(solution)/shard_map/ppermute | solution.py:703
  1049.6 70.4 %collective-permute-start.8 = (bf16[48,96,128]{2,1,0:T(8,128)(2,1)}, bf16[48,96,128]{2,1,0:T(8,128)(2,1)S(1)}, u32[]{:S(2)}, u32[]{:S(2)}) collective-permute-start(bf16[48,96,128]{2,1,0:T(8,128)(2,1)} %get-tuple-element.34), channel_id=1, source_target_pairs={{0,2},{1,3},{2,0},{3,1},{4,6},{5,7},{6,4},{7,5},{8,10},{9,11},{10,... | collective-permute-start | bytes 3538952 | tf_op jit(solution)/shard_map/ppermute | solution.py:703
  1050.9 69.1 %collective-permute-start.9 = (bf16[48,96,128]{2,1,0:T(8,128)(2,1)}, bf16[48,96,128]{2,1,0:T(8,128)(2,1)}, u32[]{:S(2)}, u32[]{:S(2)}) collective-permute-start(bf16[48,96,128]{2,1,0:T(8,128)(2,1)} %get-tuple-element.35), channel_id=1, source_target_pairs={{0,3},{1,0},{2,1},{3,2},{4,7},{5,4},{6,5},{7,6},{8,11},{9,8},{10,9... | collective-permute-start | bytes 3538952 | tf_op jit(solution)/shard_map/ppermute | solution.py:703
  1081.1 14.3 %collective-permute-start.21 = (bf16[1,3,256,128]{3,2,1,0:T(8,128)(2,1)}, bf16[1,3,256,128]{3,2,1,0:T(8,128)(2,1)S(1)}, u32[]{:S(2)}, u32[]{:S(2)}) collective-permute-start(bf16[1,3,256,128]{3,2,1,0:T(8,128)(2,1)} %get-tuple-element.77), channel_id=1, source_target_pairs={{0,4},{4,8},{8,12},{12,16},{16,20},{20,24},{24,28},{1,5},{5,9},{9,... | collective-permute-start | bytes 589832 | tf_op jit(solution)/shard_map/ppermute | solution.py:72
  1083.0 12.1 %collective-permute-start.22 = (bf16[1,3,256,128]{3,2,1,0:T(8,128)(2,1)}, bf16[1,3,256,128]{3,2,1,0:T(8,128)(2,1)S(1)}, u32[]{:S(2)}, u32[]{:S(2)}) collective-permute-start(bf16[1,3,256,128]{3,2,1,0:T(8,128)(2,1)} %get-tuple-element.76), channel_id=1, source_target_pairs={{4,0},{8,4},{12,8},{16,12},{20,16},{24,20},{28,24},{5,1},{9,5},{13... | collective-permute-start | bytes 589832 | tf_op jit(solution)/shard_map/ppermute | solution.py:72
  1095.7 21.9 %collective-permute-start.23 = (bf16[1,10,256,3]{2,3,1,0:T(4,128)(2,1)S(1)}, bf16[1,10,256,3]{2,3,1,0:T(4,128)(2,1)S(1)}, u32[]{:S(2)}, u32[]{:S(2)}) collective-permute-start(bf16[1,10,256,3]{2,3,1,0:T(4,128)(2,1)S(1)} %pad_maximum_fusion.7), channel_id=1, source_target_pairs={{0,1},{1,2},{2,3},{4,5},{5,6},{6,7},{8,9},{9,10},{10,11},{12,13},{... | collective-permute-start | bytes 46088 | tf_op jit(solution)/shard_map/ppermute | solution.py:72
  1098.9 19.9 %collective-permute-start.24 = (bf16[1,10,256,3]{2,3,1,0:T(4,128)(2,1)S(1)}, bf16[1,10,256,3]{2,3,1,0:T(4,128)(2,1)S(1)}, u32[]{:S(2)}, u32[]{:S(2)}) collective-permute-start(bf16[1,10,256,3]{2,3,1,0:T(4,128)(2,1)S(1)} %pad_maximum_fusion.8), channel_id=1, source_target_pairs={{1,0},{2,1},{3,2},{5,4},{6,5},{7,6},{9,8},{10,9},{11,10},{13,12},{... | collective-permute-start | bytes 46088 | tf_op jit(solution)/shard_map/ppermute | solution.py:72
  (37 other events, 366.6 us)
Sparse Core Ops, SparseCore 0:
  33.1 24.6 reduce-scatter.1
